TPU v7x, 32 devices: a whole 2x2x4 slice. The times are simulated.
32 devices in a mesh: dp: 4 (over x, core), ctx: 8 (over z, y).
Axes of the slice: x: 2, y: 2, z: 4, core: 2. Of those that a mesh axis runs over, the one named last changes fastest.
Arguments:
- hidden_in: bfloat16 [4, 1024, 2048], P('dp', 'ctx')
- grad_out: bfloat16 [4, 1024, 2048], P('dp', 'ctx'), may hold values from -6 to 6
- seg_len: int32 [4, 9], P('dp'), may hold values from 32 to 512, as said below
- seg_parent: int32 [4, 9], P('dp'), may hold values from 0 to 7, as said below
- gain_attn: bfloat16 [2048], replicated, may hold values from 0.5 to 1.5
- shift_attn: bfloat16 [2048], replicated, may hold values from -1 to 1
- w_qkv: bfloat16 [6144, 2048], P('ctx'), may hold values from -0.125 to 0.125
- bias_qkv: bfloat16 [6144], replicated, may hold values from -1 to 1
- w_out: bfloat16 [2048, 2048], P('ctx'), may hold values from -1 to 1
- bias_out: bfloat16 [2048], replicated, may hold values from -1 to 1
- gain_mlp: bfloat16 [2048], replicated, may hold values from 0.5 to 1.5
- shift_mlp: bfloat16 [2048], replicated, may hold values from -1 to 1
- w_up: bfloat16 [8192, 2048], P('ctx'), may hold values from -0.125 to 0.125
- bias_up: bfloat16 [8192], replicated, may hold values from -1 to 1
- w_down: bfloat16 [8192, 2048], P('ctx'), may hold values from -0.0625 to 0.0625
- bias_down: bfloat16 [2048], replicated, may hold values from -1 to 1
Outputs:
- hidden_out: bfloat16 [4, 1024, 2048], P('dp', 'ctx')
- grad_in: float32 [4, 1024, 2048], P('dp', 'ctx')
- grad_gain_attn: float32 [2048], replicated
- grad_shift_attn: float32 [2048], replicated
- grad_w_qkv: float32 [6144, 2048], P('ctx')
- grad_bias_qkv: float32 [6144], replicated
- grad_w_out: float32 [2048, 2048], P('ctx')
- grad_bias_out: float32 [2048], replicated
- grad_gain_mlp: float32 [2048], replicated
- grad_shift_mlp: float32 [2048], replicated
- grad_w_up: float32 [8192, 2048], P('ctx')
- grad_bias_up: float32 [8192], replicated
- grad_w_down: float32 [8192, 2048], P('ctx')
- grad_bias_down: float32 [2048], replicated
Inputs may be any that keep to these rules, and one draw needn't show every extreme that they name: `seg_len`: lengths of a tree's 9 segments in stored order; they sum to 1024; segment 0, the trunk, holds 256 to 512 tokens, and in every draw some tree's trunk holds exactly 512; every other segment holds 32 or more. `seg_parent`: segment 0 is its own parent; four segments are branches with parent 0; each of the four others is a leaf whose parent is a branch stored before it, one leaf to a branch.
All inputs are finite; a program needn't handle non-finite values.
Results may differ from a plain program's by a relative error of at most 0.015.
Values may be sent and summed in bfloat16 or wider, within the bound.
A program may use at most 960 MiB of HBM per device.

v0:
```python
import math

import jax
import jax.numpy as jnp
from jax import lax
from jax.sharding import PartitionSpec as P

D = 2048
HEADS = 16
HEAD_DIM = 128
ROT_DIM = 32
FF = 8192


norm_eps = 1e-05
masked_score = -1e30
block_limit = 512


def layer_norm(values, gain_vec, shift_vec):
    average = jnp.mean(values, axis=-1, keepdims=True)
    centred = values - average
    spread = jnp.mean(centred * centred, axis=-1, keepdims=True)
    return centred * lax.rsqrt(spread + norm_eps) * gain_vec + shift_vec


def tree_tables(seg_len, seg_parent):
    seg_count = seg_len.shape[0]
    seg_ends = jnp.cumsum(seg_len)
    seg_starts = seg_ends - seg_len
    labels = jnp.arange(seg_count, dtype=jnp.int32)
    parent_hit = seg_parent[:, None] == labels[None, :]
    grand_parent = jnp.sum(jnp.where(parent_hit, seg_parent[None, :], 0), axis=1)
    itself = labels[:, None] == labels[None, :]
    ancestor = itself | parent_hit | (grand_parent[:, None] == labels[None, :])
    path_start = jnp.sum(jnp.where(ancestor & jnp.logical_not(itself), seg_len[None, :], 0), axis=1)
    return (seg_ends, seg_starts, ancestor, path_start)


def rotary_tables(path_pos):
    half_dim = ROT_DIM // 2
    inverse = jnp.power(10000.0, -2.0 * jnp.arange(half_dim, dtype=jnp.float32) / ROT_DIM)
    angles = path_pos.astype(jnp.float32)[:, None] * inverse[None, :]
    angles = jnp.concatenate([angles, angles], axis=1)
    return (jnp.cos(angles), jnp.sin(angles))


def rotate(head_values, cosine, sine):
    half_dim = ROT_DIM // 2
    turned = head_values[..., :ROT_DIM]
    swapped = jnp.concatenate([-turned[..., half_dim:], turned[..., :half_dim]], axis=-1)
    mixed = turned * cosine[:, None, :] + swapped * sine[:, None, :]
    return jnp.concatenate([mixed, head_values[..., ROT_DIM:]], axis=-1)


def segment_hot(row_ids, seg_ends):
    seg_index = jnp.sum((row_ids[:, None] >= seg_ends[None, :]).astype(jnp.int32), axis=1)
    labels = jnp.arange(seg_ends.shape[0], dtype=jnp.int32)
    return (seg_index[:, None] == labels[None, :]).astype(jnp.float32)


def row_lookup(row_ids, seg_ends, ancestor_f):
    row_hot = segment_hot(row_ids, seg_ends)
    return (row_hot, jnp.dot(row_hot, ancestor_f))


def permitted(query_ids, query_reach, key_ids, key_hot):
    linked = jnp.dot(query_reach, key_hot.T) > 0.5
    return linked & (key_ids[None, :] <= query_ids[:, None])


def inner_block(row_count):
    block_rows = row_count
    while block_rows > block_limit and block_rows % 2 == 0:
        block_rows = block_rows // 2
    return block_rows


def gelu_slope(pre_act):
    normal_cdf = 0.5 * (1.0 + lax.erf(pre_act / math.sqrt(2.0)))
    return normal_cdf + pre_act * jnp.exp(-0.5 * pre_act * pre_act) / math.sqrt(2.0 * math.pi)


def body(
    hidden_in,
    grad_out,
    seg_len,
    seg_parent,
    gain_attn,
    shift_attn,
    w_qkv,
    bias_qkv,
    w_out,
    bias_out,
    gain_mlp,
    shift_mlp,
    w_up,
    bias_up,
    w_down,
    bias_down,
):
    local_rows = hidden_in.shape[1]
    scale_factor = 1.0 / math.sqrt(HEAD_DIM)
    head_shape = (local_rows, HEADS, HEAD_DIM)
    seg_ends, seg_starts, ancestor, path_start = tree_tables(seg_len[0], seg_parent[0])
    ancestor_f = ancestor.astype(jnp.float32)
    my_ids = lax.axis_index("ctx") * local_rows + jnp.arange(local_rows, dtype=jnp.int32)
    my_hot, my_reach = row_lookup(my_ids, seg_ends, ancestor_f)
    shift_table = path_start - seg_starts
    path_pos = my_ids + jnp.sum(my_hot.astype(jnp.int32) * shift_table[None, :], axis=1)
    cosine, sine = rotary_tables(path_pos)
    inputs_f = hidden_in[0].astype(jnp.float32)
    gain_a = gain_attn.astype(jnp.float32)
    shift_a = shift_attn.astype(jnp.float32)
    gain_m = gain_mlp.astype(jnp.float32)
    shift_m = shift_mlp.astype(jnp.float32)
    bias_up_f = bias_up.astype(jnp.float32)
    x_attn = layer_norm(inputs_f, gain_a, shift_a).astype(jnp.bfloat16)
    x_mlp = layer_norm(inputs_f, gain_m, shift_m).astype(jnp.bfloat16)
    qkv = jnp.einsum(
        "td,nd->tn",
        x_attn,
        lax.all_gather(w_qkv, "ctx", axis=0, tiled=True),
        preferred_element_type=jnp.float32,
    ) + bias_qkv.astype(jnp.float32)
    queries = rotate(qkv[:, :D].reshape(head_shape), cosine, sine).astype(jnp.bfloat16)
    keys_heads = rotate(qkv[:, D : 2 * D].reshape(head_shape), cosine, sine).astype(jnp.bfloat16)
    values_flat = qkv[:, 2 * D :].astype(jnp.bfloat16)
    values_heads = values_flat.reshape(head_shape)
    keys_flat = keys_heads.reshape(local_rows, D)
    queries_flat = queries.reshape(local_rows, D)

    def split_blocks(shard_pieces):
        row_count = shard_pieces[0].shape[0]
        block_rows = inner_block(row_count)
        block_count = row_count // block_rows
        shaped = tuple(
            (member.reshape(block_count, block_rows, HEADS, HEAD_DIM) for member in shard_pieces)
        )
        starts = block_rows * jnp.arange(block_count, dtype=jnp.int32)
        return shaped + (starts,)

    def attend_block(fold_state, block_items):
        key_block, value_block, block_start = block_items
        block_rows = key_block.shape[0]
        key_ids = block_start + jnp.arange(block_rows, dtype=jnp.int32)
        allowed = permitted(my_ids, my_reach, key_ids, segment_hot(key_ids, seg_ends))
        row_top, row_total, partial_value = fold_state
        scores = (
            jnp.einsum("qhd,khd->qhk", queries, key_block, preferred_element_type=jnp.float32)
            * scale_factor
        )
        scores = jnp.where(allowed[:, None, :], scores, masked_score)
        new_top = jnp.maximum(row_top, jnp.max(scores, axis=-1))
        factor = jnp.exp(row_top - new_top)
        weights = jnp.exp(scores - new_top[:, :, None])
        row_total = row_total * factor + jnp.sum(weights, axis=-1)
        partial_value = partial_value * factor[:, :, None] + jnp.einsum(
            "qhk,khd->qhd",
            weights.astype(jnp.bfloat16),
            value_block,
            preferred_element_type=jnp.float32,
        )
        fold_state = (new_top, row_total, partial_value)
        return (fold_state, None)

    start_state = (
        jnp.full((local_rows, HEADS), masked_score, jnp.float32),
        jnp.zeros((local_rows, HEADS), jnp.float32),
        jnp.zeros(head_shape, jnp.float32),
    )
    row_top, row_total, partial_value = lax.scan(
        attend_block,
        start_state,
        split_blocks(
            (
                lax.all_gather(keys_flat, "ctx", axis=0, tiled=True),
                lax.all_gather(values_flat, "ctx", axis=0, tiled=True),
            )
        ),
    )[0]
    log_total = row_top + jnp.log(row_total)
    attended_f = partial_value / row_total[:, :, None]
    attended = attended_f.reshape(local_rows, D).astype(jnp.bfloat16)
    attn_proj = jnp.einsum(
        "td,nd->tn",
        attended,
        lax.all_gather(w_out, "ctx", axis=0, tiled=True),
        preferred_element_type=jnp.float32,
    )

    def mlp_pre(up_rows):
        return (
            jnp.einsum("td,nd->tn", x_mlp, up_rows, preferred_element_type=jnp.float32) + bias_up_f
        )

    up_rows = lax.all_gather(w_up, "ctx", axis=0, tiled=True)
    down_rows = lax.all_gather(w_down, "ctx", axis=0, tiled=True)
    activated = jax.nn.gelu(mlp_pre(up_rows), approximate=False).astype(jnp.bfloat16)
    mlp_sum = jnp.dot(activated, down_rows, preferred_element_type=jnp.float32)
    bias_out_f = bias_out.astype(jnp.float32)
    bias_down_f = bias_down.astype(jnp.float32)
    hidden_out = (inputs_f + attn_proj + bias_out_f + mlp_sum + bias_down_f).astype(jnp.bfloat16)
    grad_b = grad_out[0]
    grad_f = grad_b.astype(jnp.float32)
    up_rows = lax.all_gather(w_up, "ctx", axis=0, tiled=True)
    down_rows = lax.all_gather(w_down, "ctx", axis=0, tiled=True)
    pre_act = mlp_pre(up_rows)
    activated = jax.nn.gelu(pre_act, approximate=False).astype(jnp.bfloat16)
    act_grad = jnp.einsum("td,nd->tn", grad_b, down_rows, preferred_element_type=jnp.float32)
    pre_grad = (act_grad * gelu_slope(pre_act)).astype(jnp.bfloat16)
    input_grad = jnp.dot(pre_grad, up_rows, preferred_element_type=jnp.float32)
    act_all = activated
    pre_grad_all = pre_grad
    act_all, pre_grad_all, mlp_in_grad = (act_all, pre_grad_all, input_grad)
    attended_grad = jnp.dot(
        grad_b, lax.all_gather(w_out, "ctx", axis=0, tiled=True), preferred_element_type=jnp.float32
    ).astype(jnp.bfloat16)
    attended_grad_heads = attended_grad.reshape(head_shape)
    row_delta = jnp.sum(attended_grad_heads.astype(jnp.float32) * attended_f, axis=-1)
    all_log_total, all_delta = (
        lax.all_gather(log_total, "ctx", axis=0, tiled=True),
        lax.all_gather(row_delta, "ctx", axis=0, tiled=True),
    )

    def back_block(fold_state, block_items):
        key_block, value_block, query_block, grad_block, block_start = block_items
        block_rows = key_block.shape[0]
        other_ids = block_start + jnp.arange(block_rows, dtype=jnp.int32)
        other_hot, other_reach = row_lookup(other_ids, seg_ends, ancestor_f)
        allowed_in = permitted(my_ids, my_reach, other_ids, other_hot)
        allowed_out = permitted(other_ids, other_reach, my_ids, my_hot)
        other_log = lax.dynamic_slice_in_dim(all_log_total, block_start, block_rows, 0)
        other_delta = lax.dynamic_slice_in_dim(all_delta, block_start, block_rows, 0)
        query_grad, key_grad, value_grad = fold_state
        scores = (
            jnp.einsum("qhd,khd->qhk", queries, key_block, preferred_element_type=jnp.float32)
            * scale_factor
        )
        scores = jnp.where(allowed_in[:, None, :], scores, masked_score)
        prob_mass = jnp.exp(scores - log_total[:, :, None])
        prob_grad = jnp.einsum(
            "qhd,khd->qhk", attended_grad_heads, value_block, preferred_element_type=jnp.float32
        )
        score_grad = (prob_mass * (prob_grad - row_delta[:, :, None])).astype(jnp.bfloat16)
        query_grad = (
            query_grad
            + jnp.einsum("qhk,khd->qhd", score_grad, key_block, preferred_element_type=jnp.float32)
            * scale_factor
        )
        outgoing_key_grad = key_grad
        outgoing_value_grad = value_grad
        scores = (
            jnp.einsum("qhd,khd->qhk", query_block, keys_heads, preferred_element_type=jnp.float32)
            * scale_factor
        )
        scores = jnp.where(allowed_out[:, None, :], scores, masked_score)
        prob_mass = jnp.exp(scores - other_log[:, :, None])
        outgoing_value_grad = outgoing_value_grad + jnp.einsum(
            "qhk,qhd->khd",
            prob_mass.astype(jnp.bfloat16),
            grad_block,
            preferred_element_type=jnp.float32,
        )
        prob_grad = jnp.einsum(
            "qhd,khd->qhk", grad_block, values_heads, preferred_element_type=jnp.float32
        )
        score_grad = (prob_mass * (prob_grad - other_delta[:, :, None])).astype(jnp.bfloat16)
        outgoing_key_grad = (
            outgoing_key_grad
            + jnp.einsum(
                "qhk,qhd->khd", score_grad, query_block, preferred_element_type=jnp.float32
            )
            * scale_factor
        )
        fold_state = (query_grad, outgoing_key_grad, outgoing_value_grad)
        return (fold_state, None)

    zero_heads = jnp.zeros(head_shape, jnp.float32)
    query_grad, key_grad, value_grad = lax.scan(
        back_block,
        (zero_heads, zero_heads, zero_heads),
        split_blocks(
            (
                lax.all_gather(keys_flat, "ctx", axis=0, tiled=True),
                lax.all_gather(values_flat, "ctx", axis=0, tiled=True),
                lax.all_gather(queries_flat, "ctx", axis=0, tiled=True),
                lax.all_gather(attended_grad, "ctx", axis=0, tiled=True),
            )
        ),
    )[0]

    def turn(head_values):
        return rotate(head_values, cosine, sine)

    unturn = jax.vjp(turn, zero_heads)[1]
    qkv_grad = jnp.concatenate(
        [
            unturn(query_grad)[0].reshape(local_rows, D),
            unturn(key_grad)[0].reshape(local_rows, D),
            value_grad.reshape(local_rows, D),
        ],
        axis=1,
    ).astype(jnp.bfloat16)
    attn_in_grad = jnp.dot(
        qkv_grad,
        lax.all_gather(w_qkv, "ctx", axis=0, tiled=True),
        preferred_element_type=jnp.float32,
    )
    pull_attn = jax.vjp(layer_norm, inputs_f, gain_a, shift_a)[1]
    input_part_a, gain_grad_a, shift_grad_a = pull_attn(attn_in_grad)
    pull_mlp = jax.vjp(layer_norm, inputs_f, gain_m, shift_m)[1]
    input_part_m, gain_grad_m, shift_grad_m = pull_mlp(mlp_in_grad)
    grad_in = (grad_f + input_part_a + input_part_m)[None]
    vector_sums = lax.psum(
        (
            gain_grad_a,
            shift_grad_a,
            gain_grad_m,
            shift_grad_m,
            jnp.sum(qkv_grad, axis=0, dtype=jnp.float32),
            jnp.sum(grad_f, axis=0),
            jnp.sum(pre_grad_all, axis=0, dtype=jnp.float32),
        ),
        ("dp", "ctx"),
    )
    group_count = lax.axis_size("ctx")
    section_rows = (3 * D // group_count, D // group_count, FF // group_count, FF // group_count)
    term_sources = (
        (qkv_grad, x_attn),
        (grad_b, attended),
        (pre_grad_all, x_mlp),
        (act_all, grad_b),
    )
    owner_rows = sum(section_rows)
    blocks = jnp.arange(owner_rows * lax.axis_size("ctx") // owner_rows, dtype=jnp.int32)
    parts_list = []
    for (column_source, other_side), full_rows in zip(term_sources, section_rows):
        sub_rows = full_rows // 1
        column_ids = (
            blocks[:, None] * sub_rows + jnp.arange(sub_rows, dtype=jnp.int32)[None, :]
        ).reshape(-1)
        columns = jnp.take(column_source, column_ids, axis=1)
        block_term = jnp.einsum(
            "tr,td->rd", columns, other_side, preferred_element_type=jnp.float32
        )
        parts_list.append(block_term.reshape(blocks.shape[0], sub_rows, D))
    owned_term = lax.psum_scatter(
        jnp.concatenate(parts_list, axis=1).reshape(-1, D).astype(jnp.bfloat16),
        "ctx",
        scatter_dimension=0,
        tiled=True,
    ).astype(jnp.float32)
    cut_a = section_rows[0]
    cut_b = cut_a + section_rows[1]
    cut_c = cut_b + section_rows[2]
    weight_grads = (
        lax.psum(owned_term[:cut_a].astype(jnp.bfloat16), "dp").astype(jnp.float32),
        lax.psum(owned_term[cut_a:cut_b].astype(jnp.bfloat16), "dp").astype(jnp.float32),
        lax.psum(owned_term[cut_b:cut_c].astype(jnp.bfloat16), "dp").astype(jnp.float32),
        lax.psum(owned_term[cut_c:].astype(jnp.bfloat16), "dp").astype(jnp.float32),
    )
    return (
        hidden_out[None],
        grad_in,
        vector_sums[0],
        vector_sums[1],
        weight_grads[0],
        vector_sums[4],
        weight_grads[1],
        vector_sums[5],
        vector_sums[2],
        vector_sums[3],
        weight_grads[2],
        vector_sums[6],
        weight_grads[3],
        vector_sums[5],
    )


def solution(mesh):
    placed = (
        P("dp", "ctx", None),
        P("dp", "ctx", None),
        P("dp", None),
        P("dp", None),
        P(),
        P(),
        P("ctx", None),
        P(),
        P("ctx", None),
        P(),
        P(),
        P(),
        P("ctx", None),
        P(),
        P("ctx", None),
        P(),
    )
    return jax.shard_map(
        body,
        mesh=mesh,
        in_specs=placed,
        out_specs=(
            P("dp", "ctx", None),
            P("dp", "ctx", None),
            P(),
            P(),
            P("ctx", None),
            P(),
            P("ctx", None),
            P(),
            P(),
            P(),
            P("ctx", None),
            P(),
            P("ctx", None),
            P(),
        ),
        check_vma=False,
    )
```

profile of v0, /device:TPU:13, one launch (start us, length us, event | category | flops | bytes accessed | tf_op | source)
XLA Modules:
  0.0 4313.2 jit_solution(2720108976161836193)
XLA Ops:
  8.8 124.4 %all-gather.15.cloned.1.call-done = bf16[2048,2048]{1,0:T(8,128)(2,1)} async-done(((bf16[256,2048]{1,0:T(8,128)(2,1)}), bf16[2048,2048]{1,0:T(8,128)(2,1)}) %all-gather.15.cloned.1.call-update) | async-done | bytes 8388624 | tf_op jit(solution)/shard_map/all_gather | solution.py:188
  133.2 5.4 convolution_convert_fusion.4
  140.2 475.3 %all-gather.9.cloned.1.call-done = bf16[6144,2048]{1,0:T(8,128)(2,1)} async-done(((bf16[768,2048]{1,0:T(8,128)(2,1)}), bf16[6144,2048]{1,0:T(8,128)(2,1)}) %all-gather.9.cloned.1.call-update) | async-done | bytes 25165840 | tf_op jit(solution)/shard_map/all_gather | solution.py:123
  615.5 14.4 convolution_add_fusion.1
  644.8 6.2 gather_fusion.1
  656.7 33.3 all-gather.23.cloned.1.call-done
  690.0 5.7 copy.197
  698.4 66.9 %all-gather.11.cloned.1.call-done = bf16[1024,2048]{0,1:T(8,128)(2,1)} async-done(((bf16[128,2048]{0,1:T(8,128)(2,1)}), bf16[1024,2048]{0,1:T(8,128)(2,1)}) %all-gather.11.cloned.1.call-update) | async-done | bytes 4194320 | tf_op jit(solution)/shard_map/all_gather | solution.py:177
  765.3 7.8 reshape.460
  773.1 11.2 copy.155
  784.3 55.1 %all-gather.13.cloned.1.call-done = bf16[1024,2048]{1,0:T(8,128)(2,1)} async-done(((bf16[128,2048]{1,0:T(8,128)(2,1)}), bf16[1024,2048]{1,0:T(8,128)(2,1)}) %all-gather.13.cloned.1.call-update) | async-done | bytes 4194320 | tf_op jit(solution)/shard_map/all_gather | solution.py:178
  839.4 5.6 copy.195
  845.0 69.7 %all-gather.21.cloned.1.call-done = bf16[1024,2048]{0,1:T(8,128)(2,1)} async-done(((bf16[128,2048]{0,1:T(8,128)(2,1)}), bf16[1024,2048]{0,1:T(8,128)(2,1)}) %all-gather.21.cloned.1.call-update) | async-done | bytes 4194320 | tf_op jit(solution)/shard_map/all_gather | solution.py:287
  914.7 7.8 reshape.461
  922.5 11.3 copy.166
  933.8 35.5 while.30
  935.3 4.4 fusion.278
  939.7 3.2 fusion.279
  946.3 5.1 fusion.281
  953.0 4.4 fusion.278
  957.4 3.2 fusion.279
  963.9 5.3 fusion.281
  971.7 36.3 all_gather.45
  1008.1 43.7 %all_gather.43 = f32[1024,16]{0,1:T(8,128)S(1)} all-gather(f32[128,16]{0,1:T(8,128)S(1)} %log_add_fusion), channel_id=1, replica_groups=mesh['dp'=4,'ctx'=8] {'ctx'}, dimensions={0}, use_global_device_ids=true | all-gather | bytes 73728 | tf_op jit(solution)/shard_map/all_gather | solution.py:222
  1051.8 71.5 %while.31 = (s32[]{:T(128)}, f32[128,16,128]{0,2,1:T(8,128)}, f32[128,16,128]{0,2,1:T(8,128)}, f32[128,16,128]{0,2,1:T(8,128)}, bf16[2,512,16,128]{3,1,2,0:T(8,1...) while((s32[]{:T(128)}, f32[128,16,128]{0,2,1:T(8,128)}, ...), condition=%wide.region_15.16_spmd.clone, body=%wide.region_13.15_spmd.clone.sunk | while | flops 1900784000 | bytes 69798600 | solution.py:280
  1051.8 4.5 fusion.295
  1056.3 3.6 constant_dynamic-slice_fusion.9
  1061.5 7.1 fusion.297
  1068.6 4.3 fusion.298
  1075.5 6.5 fusion.300
  1082.0 5.5 fusion.301
  1087.5 4.5 fusion.295
  1091.9 3.6 constant_dynamic-slice_fusion.9
  1097.2 7.2 fusion.297
  1104.3 4.3 fusion.298
  1111.2 6.6 fusion.300
  1117.8 5.5 fusion.301
  1128.7 22.7 gather_fusion
  1151.5 5.7 convolution_convert_fusion.3
  1157.3 3.2 broadcast_select_fusion.2
  1160.6 11.8 convolution_convert_fusion.2
  1172.4 393.0 %all-gather.17.cloned.1.call-done = bf16[8192,2048]{1,0:T(8,128)(2,1)} async-done(((bf16[1024,2048]{1,0:T(8,128)(2,1)}), bf16[8192,2048]{1,0:T(8,128)(2,1)}) %all-gather.17.cloned.1.call-update) | async-done | bytes 33554448 | tf_op jit(solution)/shard_map/all_gather | solution.py:197
  1565.4 26.5 fusion.121
  1591.9 612.8 %all-gather.19.cloned.1.call-done = bf16[8192,2048]{1,0:T(8,128)(2,1)} async-done(((bf16[1024,2048]{1,0:T(8,128)(2,1)}), bf16[8192,2048]{1,0:T(8,128)(2,1)}) %all-gather.19.cloned.1.call-update) | async-done | bytes 33554448 | tf_op jit(solution)/shard_map/all_gather | solution.py:198
  2204.7 17.7 convert_reduce_fusion.2
  2225.1 3.2 copy.174
  2228.3 29.8 gather_fusion.2
  2258.1 29.5 gather_fusion.3
  2287.6 6.2 broadcast_select_fusion.1
  2293.8 14.5 convolution_convert_fusion
  2308.3 14.6 convolution_convert_fusion.1
  2322.9 65.3 %pad_maximum_fusion = bf16[8,3072,2048]{2,1,0:T(8,128)(2,1)} fusion(bf16[8,1024,2048]{2,1,0:T(8,128)(2,1)} %convolution_convert_fusion, bf16[8,1024,2048]{2,1,0:T(8,128)(2,1)} %convolution_convert_fusion.1, bf16[8,256,2048]{2,1,0:T(8,128)(2,1)} %convolution_convert_fusion.3, bf16[8,768,2048]{2,1,0:T(8,128)(2,1)} %convolution_convert_fusion.2), kind=kLoop, calls=%fused_computation.117 | loop fusion | flops 402653184 | bytes 201326592 | tf_op jit(solution)/shard_map/concatenate | solution.py:349
  2388.3 15.0 fusion.218
  2403.4 10.8 fusion.213
  2418.2 1507.0 %reduce-scatter.2.cloned.1.call-done = bf16[3072,2048]{1,0:T(8,128)(2,1)} async-done(((bf16[24576,2048]{1,0:T(8,128)(2,1)}), bf16[3072,2048]{1,0:T(8,128)(2,1)}) %reduce-scatter.2.cloned.1.call-update) | async-done | bytes 12582928 | tf_op jit(solution)/shard_map/reduce_scatter | solution.py:348
  3925.2 6.4 fusion.214
  3931.6 4.0 slice.88
  3939.0 6.5 fusion.134
  3945.5 14.0 fusion.136
  3959.5 99.9 %all-reduce.13.cloned.1.call-done = (f32[2048]{0:T(1024)}, f32[2048]{0:T(1024)}, f32[6144]{0:T(1024)}, f32[2048]{0:T(1024)}, f32[2048]{0:T(1024)}, /*index=5*/f32[2048]{0:T(1024)}, f32[8192]{0:T(1024)}) async-done(((f32[2048]{0:T(1024)}, f32[2048]{0:T(1024)}, f32[6144]{0:T(1024)}, f32[2048]{0:T(1024)}, f32[2048]{0:T(1024)}, /*index=5*/f32[2048]{0:T(1024)}, f32[8192]{0:T(1024)}), (f32[2048]{0:T(1024)}, ...) | async-done | bytes 98320 | tf_op jit(solution)/shard_map/psum | solution.py:315
  4059.4 225.8 %all-reduce.15.cloned.1.call-done = (bf16[768,2048]{1,0:T(8,128)(2,1)}, bf16[256,2048]{1,0:T(8,128)(2,1)}, bf16[1024,2048]{1,0:T(8,128)(2,1)}, bf16[1024,2048]{1,0:T(8,128)(2,1)}) async-done(((bf16[768,2048]{1,0:T(8,128)(2,1)}, bf16[256,2048]{1,0:T(8,128)(2,1)}, bf16[1024,2048]{1,0:T(8,128)(2,1)}, bf16[1024,2048]{1,0:T(8,128)(2,1)}), (bf16[768,2048]{1,0:T(8,128)(2,1)}, bf16[256,2048]{1,0:T(8,128)(2,1)}, ...) | async-done | bytes 12582928 | tf_op jit(solution)/shard_map/psum | solution.py:358
  4285.2 5.6 convert_element_type.190
  4292.4 4.4 convert_element_type.193
  4296.9 4.4 convert_element_type.195
  (278 shorter events, 64.6 us)
Async XLA Ops:
  7.2 126.0 %copy-start.6 = (bf16[1,128,2048]{2,1,0:T(8,128)(2,1)S(1)}, bf16[1,128,2048]{2,1,0:T(8,128)(2,1)}, u32[]{:S(2)}) copy-start(bf16[1,128,2048]{2,1,0:T(8,128)(2,1)} %param.23) | copy-start | bytes 1572868
  7.2 126.0 %all-gather.15.cloned.1.call-start = ((), (), s32[]{:S(2)}) async-start(), calls=%async_computation.4 | async-start | bytes 9437184 | tf_op jit(solution)/shard_map/all_gather | solution.py:188
  7.9 607.5 %all-gather.9.cloned.1.call-start = ((), (), s32[]{:S(2)}) async-start(), calls=%async_computation.1 | async-start | bytes 28311552 | tf_op jit(solution)/shard_map/all_gather | solution.py:123
  8.7 130.0 %copy-start.45 = (bf16[6144]{0:T(1024)(128)(2,1)S(1)}, bf16[6144]{0:T(1024)(128)(2,1)}, u32[]{:S(2)}) copy-start(bf16[6144]{0:T(1024)(128)(2,1)} %param.29) | copy-start | bytes 36868
  8.7 130.0 %copy-start.50 = (bf16[2048]{0:T(1024)(128)(2,1)S(1)}, bf16[2048]{0:T(1024)(128)(2,1)}, u32[]{:S(2)}) copy-start(bf16[2048]{0:T(1024)(128)(2,1)} %param.27) | copy-start | bytes 12292
  8.7 130.0 %copy-start.51 = (bf16[2048]{0:T(1024)(128)(2,1)S(1)}, bf16[2048]{0:T(1024)(128)(2,1)}, u32[]{:S(2)}) copy-start(bf16[2048]{0:T(1024)(128)(2,1)} %param.26) | copy-start | bytes 12292
  8.7 130.1 %copy-start.56 = (s32[1,9]{1,0:T(1,128)S(1)}, s32[1,9]{1,0:T(1,128)}, u32[]{:S(2)}) copy-start(s32[1,9]{1,0:T(1,128)} %param.24) | copy-start | bytes 112
  8.7 130.3 %copy-start.59 = (s32[1,9]{1,0:T(1,128)S(1)}, s32[1,9]{1,0:T(1,128)}, u32[]{:S(2)}) copy-start(s32[1,9]{1,0:T(1,128)} %param.25) | copy-start | bytes 112
  8.7 131.0 %copy-start.4 = (bf16[1,128,2048]{2,1,0:T(8,128)(2,1)S(1)}, bf16[1,128,2048]{2,1,0:T(8,128)(2,1)}, u32[]{:S(2)}) copy-start(bf16[1,128,2048]{2,1,0:T(8,128)(2,1)} %param.22) | copy-start | bytes 1572868
  8.7 681.3 %all-gather.23.cloned.1.call-start = ((), (), s32[]{:S(2)}) async-start(), calls=%async_computation.8 | async-start | bytes 4718592 | tf_op jit(solution)/shard_map/all_gather | solution.py:288
  138.6 626.7 %all-gather.11.cloned.1.call-start = ((), (), s32[]{:S(2)}) async-start(), calls=%async_computation.2 | async-start | bytes 4718592 | tf_op jit(solution)/shard_map/all_gather | solution.py:177
  138.7 476.7 %copy-start.26 = (f32[2048]{0:T(1024)}, f32[2048]{0:T(1024)S(1)}, u32[]{:S(2)}) copy-start(f32[2048]{0:T(1024)S(1)} %convert_element_type.160) | copy-start | bytes 24580
  138.8 476.7 %copy-start.22 = (f32[2048]{0:T(1024)}, f32[2048]{0:T(1024)S(1)}, u32[]{:S(2)}) copy-start(f32[2048]{0:T(1024)S(1)} %convert_element_type.159) | copy-start | bytes 24580
  139.7 495.8 %copy-start.29 = (f32[128,32]{0,1:T(8,128)}, f32[128,32]{0,1:T(8,128)S(1)}, u32[]{:S(2)}) copy-start(f32[128,32]{0,1:T(8,128)S(1)} %get-tuple-element.612) | copy-start | bytes 49156
  139.7 495.8 %copy-start.31 = (f32[128,32]{0,1:T(8,128)}, f32[128,32]{0,1:T(8,128)S(1)}, u32[]{:S(2)}) copy-start(f32[128,32]{0,1:T(8,128)S(1)} %get-tuple-element.613) | copy-start | bytes 49156
  139.9 490.0 %copy-start.37 = (f32[128]{0:T(128)}, f32[128]{0:T(128)S(1)}, u32[]{:S(2)}) copy-start(f32[128]{0:T(128)S(1)} %broadcast_multiply_fusion.1) | copy-start | bytes 1540
  140.2 489.7 %copy-start.57 = (f32[128]{0:T(128)}, f32[128]{0:T(128)S(1)}, u32[]{:S(2)}) copy-start(f32[128]{0:T(128)S(1)} %fusion.156) | copy-start | bytes 1540
  140.2 489.7 %copy-start.42 = (f32[128]{0:T(128)}, f32[128]{0:T(128)S(1)}, u32[]{:S(2)}) copy-start(f32[128]{0:T(128)S(1)} %fusion.207) | copy-start | bytes 1540
  637.4 202.0 %all-gather.13.cloned.1.call-start = ((), (), s32[]{:S(2)}) async-start(), calls=%async_computation.3 | async-start | bytes 4718592 | tf_op jit(solution)/shard_map/all_gather | solution.py:178
  639.5 275.1 %all-gather.21.cloned.1.call-start = ((), (), s32[]{:S(2)}) async-start(), calls=%async_computation.7 | async-start | bytes 4718592 | tf_op jit(solution)/shard_map/all_gather | solution.py:287
  640.6 924.9 %all-gather.17.cloned.1.call-start = ((), (), s32[]{:S(2)}) async-start(), calls=%async_computation.5 | async-start | bytes 37748736 | tf_op jit(solution)/shard_map/all_gather | solution.py:197
  641.3 1563.4 %all-gather.19.cloned.1.call-start = ((), (), s32[]{:S(2)}) async-start(), calls=%async_computation.6 | async-start | bytes 37748736 | tf_op jit(solution)/shard_map/all_gather | solution.py:198
  642.1 12.3 copy-start.10
  642.1 3283.2 %reduce-scatter.2.cloned.1.call-start = ((), (), s32[]{:S(2)}) async-start(), calls=%async_computation.9 | async-start | bytes 113246208 | tf_op jit(solution)/shard_map/reduce_scatter | solution.py:348
  690.0 5.7 copy-start.15
  690.0 5.9 copy-start.14
  1051.8 4.5 copy-start.3
  1087.5 4.5 copy-start.3
  1123.3 3.9 copy-start.19
  1123.3 3.9 copy-start.20
  1123.3 3.9 copy-start.32
  1123.3 4.0 copy-start.30
  1128.7 22.7 copy-start
  1128.7 22.7 copy-start.12
  1128.7 22.7 copy-start.18
  1151.4 5.8 copy-start.11
  1151.5 5.8 copy-start.41
  1151.5 9.0 copy-start.5
  1151.5 9.0 copy-start.23
  1151.5 9.0 copy-start.27
  1151.5 9.0 copy-start.38
  1151.5 9.0 copy-start.43
  1160.5 404.9 %copy-start.28 = (f32[2048]{0:T(1024)S(1)}, f32[2048]{0:T(1024)}, u32[]{:S(2)}) copy-start(f32[2048]{0:T(1024)} %convert_element_type.172) | copy-start | bytes 24580
  1160.5 404.9 %copy-start.34 = (f32[8192]{0:T(1024)S(1)}, f32[8192]{0:T(1024)}, u32[]{:S(2)}) copy-start(f32[8192]{0:T(1024)} %convert_element_type.175) | copy-start | bytes 98308
  1160.5 404.9 %copy-start.39 = (f32[2048]{0:T(1024)S(1)}, f32[2048]{0:T(1024)}, u32[]{:S(2)}) copy-start(f32[2048]{0:T(1024)} %convert_element_type.173) | copy-start | bytes 24580
  1172.4 1032.3 %copy-start.7 = (bf16[1,128,2048]{2,1,0:T(8,128)(2,1)S(1)}, bf16[1,128,2048]{2,1,0:T(8,128)(2,1)}, u32[]{:S(2)}) copy-start(bf16[1,128,2048]{2,1,0:T(8,128)(2,1)} %param.23) | copy-start | bytes 1572868
  2222.4 5.9 copy-start.25
  2258.1 29.5 copy-start.33
  2388.3 15.1 copy-start.1
  2388.3 15.1 copy-start.24
  2388.3 1671.1 %all-reduce.13.cloned.1.call-start = ((), (), s32[]{:S(2)}) async-start(), calls=%async_computation.10 | async-start | bytes 196608 | tf_op jit(solution)/shard_map/psum | solution.py:315
  2403.4 10.9 copy-start.58
  2418.1 1867.1 %all-reduce.15.cloned.1.call-start = ((), (), s32[]{:S(2)}) async-start(), calls=%async_computation.11 | async-start | bytes 25165824 | tf_op jit(solution)/shard_map/psum | solution.py:358
  3939.0 6.5 copy-start.8
  4285.2 5.6 copy-start.21
  4285.2 7.2 copy-start.17
  4292.4 4.5 copy-start.16
  4296.8 4.5 copy-start.36
  4296.8 5.1 copy-start.49
  4296.8 5.7 copy-start.48
  4296.8 6.3 copy-start.40
  4296.8 7.5 copy-start.47
  4296.8 8.1 copy-start.46
  4296.9 8.7 copy-start.35
  (9 other events, 19.4 us)
Sparse Core Ops, SparseCore 0:
  10.2 122.9 all-gather.14
  134.7 480.7 all-gather.8
  618.2 71.7 all-gather.22
  692.5 72.7 all-gather.10
  767.3 72.0 all-gather.12
  841.9 72.7 all-gather.20
  916.2 649.1 all-gather.16
  1567.0 637.6 all-gather.18
  2388.4 1536.7 reduce-scatter.1
  3933.8 125.6 all-reduce.12
  4063.3 221.8 all-reduce.14
where the time goes:
time: 4320 us; the launch traced here: 4310 us
  waiting for transfers between devices  3670 us (85%)
  matrix products  234 us (5%)
  local copies, waits for them, and re-layouts  193 us (4%)
  other arithmetic  119 us (3%)
  blocking collectives  80 us (2%)
    reduce_scatter x1, waiting for transfers between devices, body(): lax.psum_scatter(jnp.concatenate(parts_list, axis=1).reshape(-1, D).astyp...  1510 us
    all_gather x1, waiting for transfers between devices, body(): down_rows = lax.all_gather(w_down, 'ctx', axis=0, tiled=True)  613 us
    all_gather x1, waiting for transfers between devices, body(): lax.all_gather(w_qkv, 'ctx', axis=0, tiled=True)  475 us
    all_gather x1, waiting for transfers between devices, body(): up_rows = lax.all_gather(w_up, 'ctx', axis=0, tiled=True)  393 us
    psum x1, waiting for transfers between devices, body(): lax.psum(owned_term[:cut_a].astype(jnp.bfloat16), 'dp').astype(jnp.float32)  226 us
    all_gather x1, waiting for transfers between devices, body(): lax.all_gather(w_out, 'ctx', axis=0, tiled=True)  124 us
    psum x1, waiting for transfers between devices, body(): lax.psum((gain_grad_a, shift_grad_a, gain_grad_m, shift_grad_m, jnp.sum(q...  99.9 us
    gather x4, local copies, waits for them, and re-layouts, body(): columns = jnp.take(column_source, column_ids, axis=1)  88.2 us
  transfers between devices with their start and end apart: 11, of which 11 were waited for; matrix products, arithmetic and copies ran while one was open for 8% of the time, Pallas kernels for 0%

commit v1 on v0

--- a/solution.py
+++ b/solution.py
@@ -11,24 +11,18 @@
 ROT_DIM = 32
 FF = 8192
 
-
 norm_eps = 1e-05
 masked_score = -1e30
-block_limit = 512
-
-
-def layer_norm(values, gain_vec, shift_vec):
-    average = jnp.mean(values, axis=-1, keepdims=True)
-    centred = values - average
-    spread = jnp.mean(centred * centred, axis=-1, keepdims=True)
-    return centred * lax.rsqrt(spread + norm_eps) * gain_vec + shift_vec
+f32 = jnp.float32
+bf16 = jnp.bfloat16
 
 
 def tree_tables(seg_len, seg_parent):
     seg_count = seg_len.shape[0]
-    seg_ends = jnp.cumsum(seg_len)
-    seg_starts = seg_ends - seg_len
     labels = jnp.arange(seg_count, dtype=jnp.int32)
+    earlier = labels[:, None] > labels[None, :]
+    seg_starts = jnp.sum(jnp.where(earlier, seg_len[None, :], 0), axis=1)
+    seg_ends = seg_starts + seg_len
     parent_hit = seg_parent[:, None] == labels[None, :]
     grand_parent = jnp.sum(jnp.where(parent_hit, seg_parent[None, :], 0), axis=1)
     itself = labels[:, None] == labels[None, :]
@@ -39,8 +33,8 @@
 
 def rotary_tables(path_pos):
     half_dim = ROT_DIM // 2
-    inverse = jnp.power(10000.0, -2.0 * jnp.arange(half_dim, dtype=jnp.float32) / ROT_DIM)
-    angles = path_pos.astype(jnp.float32)[:, None] * inverse[None, :]
+    inverse = jnp.power(10000.0, -2.0 * jnp.arange(half_dim, dtype=f32) / ROT_DIM)
+    angles = path_pos.astype(f32)[:, None] * inverse[None, :]
     angles = jnp.concatenate([angles, angles], axis=1)
     return (jnp.cos(angles), jnp.sin(angles))
 
@@ -53,6 +47,221 @@
     return jnp.concatenate([mixed, head_values[..., ROT_DIM:]], axis=-1)
 
 
+def gelu_slope(pre_act):
+    normal_cdf = 0.5 * (1.0 + lax.erf(pre_act / math.sqrt(2.0)))
+    return normal_cdf + pre_act * jnp.exp(-0.5 * pre_act * pre_act) / math.sqrt(2.0 * math.pi)
+
+
+def dot_nt(a, b):
+    return lax.dot_general(a, b, (((1,), (1,)), ((), ())), preferred_element_type=f32)
+
+
+def dot_nn(a, b):
+    return lax.dot_general(a, b, (((1,), (0,)), ((), ())), preferred_element_type=f32)
+
+
+def dot_tn(a, b):
+    return lax.dot_general(a, b, (((0,), (0,)), ((), ())), preferred_element_type=f32)
+
+
+def body(
+    hidden_in,
+    grad_out,
+    seg_len,
+    seg_parent,
+    gain_attn,
+    shift_attn,
+    w_qkv,
+    bias_qkv,
+    w_out,
+    bias_out,
+    gain_mlp,
+    shift_mlp,
+    w_up,
+    bias_up,
+    w_down,
+    bias_down,
+):
+    group = lax.axis_size("ctx")
+    me = lax.axis_index("ctx")
+    local_rows = hidden_in.shape[1]
+    tokens = local_rows * group
+    head_count = HEADS // group
+    head_cols = head_count * HEAD_DIM
+    head_shape = (tokens, head_count, HEAD_DIM)
+    scale = 1.0 / math.sqrt(HEAD_DIM)
+
+    hidden_all = lax.all_gather(hidden_in[0], "ctx", axis=0, tiled=True)
+    grad_all = lax.all_gather(grad_out[0], "ctx", axis=0, tiled=True)
+
+    blocks = w_qkv.reshape(3, head_cols, D)
+    arrived = jnp.stack(
+        [
+            lax.ppermute(blocks[j], "ctx", [(c, (3 * c + j) % group) for c in range(group)])
+            for j in range(3)
+        ]
+    )
+    slots = [(kind * group + me) % 3 for kind in range(3)]
+    w_heads = [lax.dynamic_index_in_dim(arrived, slot, 0, keepdims=False) for slot in slots]
+    w_out_cols = lax.all_to_all(
+        w_out, "ctx", split_axis=1, concat_axis=0, tiled=True
+    )
+
+    seg_ends, seg_starts, ancestor, path_start = tree_tables(seg_len[0], seg_parent[0])
+    ids = jnp.arange(tokens, dtype=jnp.int32)
+    seg_index = jnp.sum((ids[:, None] >= seg_ends[None, :]).astype(jnp.int32), axis=1)
+    labels = jnp.arange(seg_ends.shape[0], dtype=jnp.int32)
+    hot = (seg_index[:, None] == labels[None, :]).astype(f32)
+    reach = jnp.dot(hot, ancestor.astype(f32))
+    path_pos = ids + jnp.sum(hot.astype(jnp.int32) * (path_start - seg_starts)[None, :], axis=1)
+    cosine, sine = rotary_tables(path_pos)
+    allowed = (jnp.dot(reach, hot.T) > 0.5) & (ids[None, :] <= ids[:, None])
+
+    gain_a = gain_attn.astype(f32)
+    gain_m = gain_mlp.astype(f32)
+    hid = hidden_all.astype(f32)
+    mean = jnp.mean(hid, axis=-1, keepdims=True)
+    centred = hid - mean
+    rstd = lax.rsqrt(jnp.mean(centred * centred, axis=-1, keepdims=True) + norm_eps)
+    normed = centred * rstd
+    x_attn = (normed * gain_a + shift_attn.astype(f32)).astype(bf16)
+    x_mlp = (normed * gain_m + shift_mlp.astype(f32)).astype(bf16)
+
+    my_bias = [
+        lax.dynamic_slice_in_dim(bias_qkv, kind * D + me * head_cols, head_cols).astype(f32)
+        for kind in range(3)
+    ]
+    q_raw, k_raw, v_raw = [
+        (dot_nt(x_attn, w_heads[kind]) + my_bias[kind]).reshape(head_shape) for kind in range(3)
+    ]
+    q = rotate(q_raw, cosine, sine).astype(bf16)
+    k = rotate(k_raw, cosine, sine).astype(bf16)
+    v = v_raw.astype(bf16)
+    scores = jnp.einsum("qhd,khd->hqk", q, k, preferred_element_type=f32) * scale
+    scores = jnp.where(allowed[None], scores, masked_score)
+    top = jnp.max(scores, axis=-1, keepdims=True)
+    expo = jnp.exp(scores - top)
+    probs = expo / jnp.sum(expo, axis=-1, keepdims=True)
+    weights = probs.astype(bf16)
+    attended = jnp.einsum("hqk,khd->qhd", weights, v, preferred_element_type=f32).astype(bf16)
+    attended = attended.reshape(tokens, head_cols)
+
+    up_bias = lax.dynamic_slice_in_dim(bias_up, me * w_up.shape[0], w_up.shape[0]).astype(f32)
+    pre_act = dot_nt(x_mlp, w_up) + up_bias
+    act = jax.nn.gelu(pre_act, approximate=False).astype(bf16)
+    partial = dot_nt(attended, w_out_cols) + dot_nn(act, w_down)
+    summed = lax.psum_scatter(partial.astype(bf16), "ctx", scatter_dimension=0, tiled=True)
+    hidden_out = (
+        hidden_in[0].astype(f32) + summed.astype(f32) + bias_out.astype(f32) + bias_down.astype(f32)
+    ).astype(bf16)
+
+    grad_w_down = dot_tn(act, grad_all).astype(bf16)
+    pre_grad = (dot_nt(grad_all, w_down) * gelu_slope(pre_act)).astype(bf16)
+    grad_w_up = dot_tn(pre_grad, x_mlp).astype(bf16)
+    mlp_in_grad = dot_nn(pre_grad, w_up)
+
+    grad_w_out_cols = dot_tn(grad_all, attended).astype(bf16)
+    att_grad = dot_nn(grad_all, w_out_cols).astype(bf16).reshape(head_shape)
+    prob_grad = jnp.einsum("qhd,khd->hqk", att_grad, v, preferred_element_type=f32)
+    delta = jnp.sum(probs * prob_grad, axis=-1, keepdims=True)
+    score_grad = (probs * (prob_grad - delta)).astype(bf16)
+    q_grad = jnp.einsum("hqk,khd->qhd", score_grad, k, preferred_element_type=f32) * scale
+    k_grad = jnp.einsum("hqk,qhd->khd", score_grad, q, preferred_element_type=f32) * scale
+    v_grad = jnp.einsum("hqk,qhd->khd", weights, att_grad, preferred_element_type=f32)
+    qkv_grad = [
+        rotate(q_grad, cosine, -sine).astype(bf16).reshape(tokens, head_cols),
+        rotate(k_grad, cosine, -sine).astype(bf16).reshape(tokens, head_cols),
+        v_grad.astype(bf16).reshape(tokens, head_cols),
+    ]
+    attn_in_grad = sum(dot_nn(qkv_grad[kind], w_heads[kind]) for kind in range(3))
+    grad_heads = jnp.stack([dot_tn(qkv_grad[kind], x_attn).astype(bf16) for kind in range(3)])
+
+    back = attn_in_grad * gain_a + mlp_in_grad * gain_m
+    w_sum = lax.psum_scatter(back.astype(bf16), "ctx", scatter_dimension=0, tiled=True).astype(f32)
+    start = me * local_rows
+    my_rstd = lax.dynamic_slice_in_dim(rstd, start, local_rows)
+    my_normed = (
+        hidden_in[0].astype(f32) - lax.dynamic_slice_in_dim(mean, start, local_rows)
+    ) * my_rstd
+    grad_f = grad_out[0].astype(f32)
+    grad_in = (
+        grad_f
+        + (
+            w_sum
+            - jnp.mean(w_sum, axis=-1, keepdims=True)
+            - my_normed * jnp.mean(w_sum * my_normed, axis=-1, keepdims=True)
+        )
+        * my_rstd
+    )
+
+    def widen(part, length, at):
+        return lax.dynamic_update_slice(jnp.zeros((length,), f32), part, (at,))
+
+    bias_qkv_grad = jnp.concatenate(
+        [
+            widen(jnp.sum(qkv_grad[kind], axis=0, dtype=f32), D, me * head_cols)
+            for kind in range(3)
+        ]
+    )
+    vectors = jnp.concatenate(
+        [
+            jnp.sum(attn_in_grad * normed, axis=0),
+            jnp.sum(attn_in_grad, axis=0),
+            jnp.sum(mlp_in_grad * normed, axis=0),
+            jnp.sum(mlp_in_grad, axis=0),
+            bias_qkv_grad,
+            jnp.sum(grad_f, axis=0),
+            widen(jnp.sum(pre_grad, axis=0, dtype=f32), FF, me * w_up.shape[0]),
+        ]
+    )
+    vectors = lax.psum(vectors, ("dp", "ctx"))
+    cuts = [D, D, D, D, 3 * D, D, FF]
+    ends = [sum(cuts[: i + 1]) for i in range(len(cuts))]
+    gain_grad_a, shift_grad_a, gain_grad_m, shift_grad_m, qkv_bias_grad, out_bias_grad, up_bias_grad = [
+        vectors[end - cut : end] for cut, end in zip(cuts, ends)
+    ]
+
+    returned = []
+    for j in range(3):
+        kind_of_slot = sum(
+            kind * ((kind * group + me) % 3 == j).astype(jnp.int32) for kind in range(3)
+        )
+        block = lax.dynamic_index_in_dim(grad_heads, kind_of_slot, 0, keepdims=False)
+        returned.append(
+            lax.ppermute(block, "ctx", [((3 * c + j) % group, c) for c in range(group)])
+        )
+    grad_w_qkv = jnp.concatenate(returned, axis=0)
+    grad_w_out = lax.all_to_all(
+        grad_w_out_cols, "ctx", split_axis=0, concat_axis=1, tiled=True
+    )
+    return (
+        hidden_out[None],
+        grad_in[None],
+        gain_grad_a,
+        shift_grad_a,
+        lax.psum(grad_w_qkv, "dp").astype(f32),
+        qkv_bias_grad,
+        lax.psum(grad_w_out, "dp").astype(f32),
+        out_bias_grad,
+        gain_grad_m,
+        shift_grad_m,
+        lax.psum(grad_w_up, "dp").astype(f32),
+        up_bias_grad,
+        lax.psum(grad_w_down, "dp").astype(f32),
+        out_bias_grad,
+    )
+
+
+block_limit = 512
+
+
+def layer_norm(values, gain_vec, shift_vec):
+    average = jnp.mean(values, axis=-1, keepdims=True)
+    centred = values - average
+    spread = jnp.mean(centred * centred, axis=-1, keepdims=True)
+    return centred * lax.rsqrt(spread + norm_eps) * gain_vec + shift_vec
+
+
 def segment_hot(row_ids, seg_ends):
     seg_index = jnp.sum((row_ids[:, None] >= seg_ends[None, :]).astype(jnp.int32), axis=1)
     labels = jnp.arange(seg_ends.shape[0], dtype=jnp.int32)
@@ -76,12 +285,7 @@
     return block_rows
 
 
-def gelu_slope(pre_act):
-    normal_cdf = 0.5 * (1.0 + lax.erf(pre_act / math.sqrt(2.0)))
-    return normal_cdf + pre_act * jnp.exp(-0.5 * pre_act * pre_act) / math.sqrt(2.0 * math.pi)
-
-
-def body(
+def gather_body(
     hidden_in,
     grad_out,
     seg_len,
@@ -379,42 +583,43 @@
 
 
 def solution(mesh):
-    placed = (
-        P("dp", "ctx", None),
-        P("dp", "ctx", None),
-        P("dp", None),
-        P("dp", None),
-        P(),
-        P(),
-        P("ctx", None),
-        P(),
-        P("ctx", None),
-        P(),
-        P(),
-        P(),
-        P("ctx", None),
-        P(),
-        P("ctx", None),
-        P(),
-    )
+    token = P("dp", "ctx", None)
+    rows = P("ctx", None)
     return jax.shard_map(
-        body,
+        body if HEADS % mesh.shape["ctx"] == 0 else gather_body,
         mesh=mesh,
-        in_specs=placed,
+        in_specs=(
+            token,
+            token,
+            P("dp", None),
+            P("dp", None),
+            P(),
+            P(),
+            rows,
+            P(),
+            rows,
+            P(),
+            P(),
+            P(),
+            rows,
+            P(),
+            rows,
+            P(),
+        ),
         out_specs=(
-            P("dp", "ctx", None),
-            P("dp", "ctx", None),
-            P(),
-            P(),
-            P("ctx", None),
-            P(),
-            P("ctx", None),
-            P(),
-            P(),
-            P(),
-            P("ctx", None),
-            P(),
-            P("ctx", None),
+            token,
+            token,
+            P(),
+            P(),
+            rows,
+            P(),
+            rows,
+            P(),
+            P(),
+            P(),
+            rows,
+            P(),
+            rows,
             P(),
         ),
         check_vma=False,

time: 4320 us -> 910 us (0.21)
  waiting for transfers between devices: 3670 us -> 632 us
  local copies, waits for them, and re-layouts: 193 us -> 45.1 us
  matrix products: 234 us -> 121 us
  blocking collectives: 80 us -> 0 us
  other arithmetic: 119 us -> 50.6 us
    all_gather x8 -> x2, waiting for transfers between devices: 1830 us -> 23 us  [the longest x1 23 us: body(): grad_all = lax.all_gather(grad_out[0], 'ctx', axis=0, tiled=True)]
    reduce_scatter x1 -> x2, waiting for transfers between devices: 1510 us -> 167 us  [the longest x1 90.2 us: body(): lax.psum_scatter(partial.astype(bf16), 'ctx', scatter_dimension=0, tiled=...]
    ppermute x0 -> x6, waiting for transfers between devices: none -> 128 us  [the longest x3 110 us: body(): lax.ppermute(blocks[j], 'ctx', [(c, (3 * c + j) % group) for c in range(g...]
    dot_general x33 -> x24, matrix products: 234 us -> 111 us  [the longest x6 37.8 us: dot_nn(): lax.dot_general(a, b, (((1,), (0,)), ((), ())), preferred_element_type=f32)]
    gather x4 -> x0, local copies, waits for them, and re-layouts: 88.2 us -> none  [body(): columns = jnp.take(column_source, column_ids, axis=1)]
    all_gather x2 -> x0, blocking collectives: 80 us -> none  [the longest x1 43.7 us: body(): lax.all_gather(log_total, 'ctx', axis=0, tiled=True)]
    concatenate x1 -> x3, other arithmetic: 65.3 us -> 3.88 us  [the longest x1 3.14 us: body(): grad_w_qkv = jnp.concatenate(returned, axis=0)]
  transfers between devices with their start and end apart: 11 -> 14, of which waited for: 11 -> 9; matrix products, arithmetic and copies ran while one was open for 8% -> 15% of each run, Pallas kernels for 0% -> 0%
where the time goes in v1:
time: 910 us; the launch traced here: 901 us
  waiting for transfers between devices  632 us (69%)
  matrix products  121 us (13%)
  other arithmetic  50.6 us (6%)
  local copies, waits for them, and re-layouts  45.1 us (5%)
  starting transfers between devices  37.3 us (4%)
  between operations  15.4 us (2%)
    psum x1, waiting for transfers between devices, body(): lax.psum(grad_w_qkv, 'dp').astype(f32)  222 us
    ppermute x3, waiting for transfers between devices, body(): lax.ppermute(blocks[j], 'ctx', [(c, (3 * c + j) % group) for c in range(g...  110 us
    psum x1, waiting for transfers between devices, body(): vectors = lax.psum(vectors, ('dp', 'ctx'))  90.6 us
    reduce_scatter x1, waiting for transfers between devices, body(): lax.psum_scatter(partial.astype(bf16), 'ctx', scatter_dimension=0, tiled=...  90.2 us
    reduce_scatter x1, waiting for transfers between devices, body(): lax.psum_scatter(back.astype(bf16), 'ctx', scatter_dimension=0, tiled=True)  76.5 us
    dot_general x6, matrix products, dot_nn(): lax.dot_general(a, b, (((1,), (0,)), ((), ())), preferred_element_type=f32)  37.8 us
    dot_general x6, matrix products, dot_tn(): lax.dot_general(a, b, (((0,), (0,)), ((), ())), preferred_element_type=f32)  30.7 us
    dot_general x6, matrix products, dot_nt(): lax.dot_general(a, b, (((1,), (1,)), ((), ())), preferred_element_type=f32)  29 us
  transfers between devices with their start and end apart: 14, of which 9 were waited for; matrix products, arithmetic and copies ran while one was open for 15% of the time, Pallas kernels for 0%

profile of v1, /device:TPU:13, one launch (start us, length us, event | category | flops | bytes accessed | tf_op | source)
XLA Modules:
  0.0 901.0 jit_solution(14777632967265698385)
XLA Ops:
  7.9 2.5 copy.138
  10.4 5.8 all-to-all-start
  16.2 1.7 fusion.127
  18.0 2.2 collective-permute-start
  20.1 9.5 %collective-permute-start.2 = (bf16[256,2048]{1,0:T(8,128)(2,1)}, bf16[256,2048]{1,0:T(8,128)(2,1)}, u32[]{:S(2)}, u32[]{:S(2)}) collective-permute-start(bf16[256,2048]{1,0:T(8,128)(2,1)} %get-tuple-element.37), channel_id=1, source_target_pairs={{0,2},{1,5},{2,0},{3,3},{4,6},{5,1},{6,4},{7,7},{8,10},{9,13},{10,... | collective-permute-start | bytes 3145736 | tf_op jit(solution)/shard_map/ppermute | solution.py:100
  36.0 2.6 copy.128
  41.9 106.8 %collective-permute-done = bf16[256,2048]{1,0:T(8,128)(2,1)S(1)} collective-permute-done((bf16[256,2048]{1,0:T(8,128)(2,1)}, bf16[256,2048]{1,0:T(8,128)(2,1)S(1)}, u32[]{:S(2)}, u32[]{:S(2)}) %collective-permute-start) | collective-permute-done | bytes 1048608 | tf_op jit(solution)/shard_map/ppermute | solution.py:100
  148.7 3.2 collective-permute-done.1
  151.9 2.2 pad_maximum_fusion
  154.1 3.0 copy.139
  157.1 3.0 convert_reduce_fusion
  161.8 2.1 fusion.9
  169.3 2.0 copy.167
  173.0 2.3 copy.135
  175.3 2.3 copy.166
  180.9 2.3 copy.164
  183.2 3.9 add_convert_fusion.3
  187.1 2.1 fusion.61
  189.2 9.3 %fusion.129 = (f32[2,1024]{1,0:T(2,128)S(1)}, f32[2,1024,1024]{1,2,0:T(8,128)}) fusion(pred[1024,1024]{0,1:T(8,128)(4,1)} %copy.128, bf16[1024,2,96]{2,0,1:T(8,128)(2,1)} %copy.167, bf16[1024,2,32]{2,0,1:T(8,128)(2,1)} %get-tuple-element.46, bf16[1024,2,96]{2,0,1:T(8,128)(2,1)} %copy.165, bf16[1024,2,32]{2,0,1:T(8,128)(2,1)} %get-tuple-element.45), kind=kOutput, calls=%fused_computation.210 | convolution fusion | flops 547357696 | bytes 10493952 | tf_op jit(solution)/shard_map/sub | solution.py:143
  198.5 5.1 fusion.62
  203.6 23.0 %all-gather.7.cloned.1.call-done = bf16[1,1024,2048]{2,1,0:T(8,128)(2,1)} async-done(((bf16[1,128,2048]{2,1,0:T(8,128)(2,1)}), bf16[1,1024,2048]{2,1,0:T(8,128)(2,1)}) %all-gather.7.cloned.1.call-update) | async-done | bytes 4194320 | tf_op jit(solution)/shard_map/all_gather | solution.py:95
  226.7 3.9 fusion.68
  231.6 2.4 convert_reduce_fusion.4
  234.0 2.0 multiply_reduce_fusion
  236.0 2.5 multiply_convert_fusion
  239.9 2.0 fusion.60
  243.9 1.6 convert_reduce_fusion.5
  245.5 2.0 copy.150
  247.6 4.6 fusion.51
  252.2 4.6 fusion.85
  256.8 2.0 copy.146
  258.8 4.7 fusion.50
  263.6 5.5 fusion.88
  269.9 14.9 %fusion.18 = (bf16[1024,1024]{1,0:T(8,128)(2,1)}, f32[1024,1024]{1,0:T(8,128)S(1)}) fusion(f32[1024]{0:T(1024)S(1)} %copy-done.41, bf16[1024,2048]{1,0:T(8,128)(2,1)S(1)} %copy-done.45, bf16[1,1024,2048]{2,1,0:T(8,128)(2,1)S(1)} %copy-done.1, f32[2048]{0:T(1024)S(1)} %copy-done.34, f32[2048]{0:T(1024)S(1)} %copy-done.33, f32[1024]{0:T(1024)S(1)} %add_rsqrt_fusion, ...), kind=kOutput, calls=%fused_computation.29 | convolution fusion | flops 4376756224 | bytes 14708736 | tf_op jit(solution)/shard_map/dot_general | solution.py:56
  284.8 6.1 convert_reduce_fusion.1
  291.0 6.9 fusion.131
  300.3 5.7 all-to-all-start.1
  306.0 3.6 fusion.52
  309.6 1.7 pad_maximum_fusion.1
  311.3 1.8 dynamic-slice_bitcast_fusion.2
  313.2 2.3 collective-permute-start.3
  315.5 9.5 %collective-permute-start.5 = (bf16[256,2048]{1,0:T(8,128)(2,1)}, bf16[256,2048]{1,0:T(8,128)(2,1)}, u32[]{:S(2)}, u32[]{:S(2)}) collective-permute-start(bf16[256,2048]{1,0:T(8,128)(2,1)} %get-tuple-element.34), channel_id=1, source_target_pairs={{2,0},{5,1},{0,2},{3,3},{6,4},{1,5},{4,6},{7,7},{10,8},{13,9},{8,1... | collective-permute-start | bytes 3145736 | tf_op jit(solution)/shard_map/ppermute | solution.py:231
  324.9 2.2 collective-permute-start.4
  327.1 9.9 %fusion.125 = (f32[2048]{0:T(1024)S(1)}, f32[2048]{0:T(1024)S(1)}, bf16[1024,2048]{1,0:T(8,128)(2,1)}, f32[2048]{0:T(1024)S(1)}, f32[2048]{0:T(1024)S(1)}) fusion(f32[1024,2048]{1,0:T(8,128)} %fusion.131, f32[1024]{0:T(1024)S(1)} %add_rsqrt_fusion, f32[1024]{0:T(1024)S(1)} %broadcast_multiply_fusion.1, bf16[1,1024,2048]{2,1,0:T(8,128)(2,1)S(1)} %copy-done.2, ...), kind=kOutput, calls=%fused_computation.206 | convolution fusion | flops 1105190912 | bytes 35184644 | tf_op jit(solution)/shard_map/dot_general | solution.py:60
  338.4 10.0 %convolution_convert_fusion = bf16[1024,2048]{1,0:T(8,128)(2,1)} fusion(bf16[1024,1024]{1,0:T(8,128)(2,1)} %copy-done.51, bf16[1,1024,2048]{2,1,0:T(8,128)(2,1)} %all-gather.5.cloned.1.call-done, f32[2048]{0:T(1024)S(1)} %copy-done.34, f32[2048]{0:T(1024)S(1)} %copy-done.33, f32[1024]{0:T(1024)S(1)} %add_rsqrt_fusion, f32[1024]{0:T(1024)S(1)} %broadcast_multiply_fusion.1), kind=kOutput, calls=%fused_computation.67 | convolution fusion | flops 4309647360 | bytes 10510336 | tf_op jit(solution)/shard_map/dot_general | solution.py:64
  348.5 6.4 fusion.44
  354.9 8.8 collective-permute-done.3
  363.7 9.7 %collective-permute-done.4 = bf16[256,2048]{1,0:T(8,128)(2,1)} collective-permute-done((bf16[256,2048]{1,0:T(8,128)(2,1)}, bf16[256,2048]{1,0:T(8,128)(2,1)}, u32[]{:S(2)}, u32[]{:S(2)}) %collective-permute-start.4) | collective-permute-done | bytes 1048608 | tf_op jit(solution)/shard_map/ppermute | solution.py:231
  373.3 3.1 pad_maximum_fusion.2
  376.5 1.4 copy.153
  378.6 7.1 fusion.130
  385.7 3.3 add_convert_fusion.1
  389.8 90.6 %all-reduce.4.cloned.1.call-done = f32[24576]{0:T(1024)} async-done(((f32[24576]{0:T(1024)}), f32[24576]{0:T(1024)}) %all-reduce.4.cloned.1.call-update) | async-done | bytes 98320 | tf_op jit(solution)/shard_map/psum | solution.py:217
  480.4 1.4 fusion.128
  483.2 1.4 slice.139
  484.5 222.0 %all-reduce.6.cloned.1.call-done = (bf16[768,2048]{1,0:T(8,128)(2,1)}, bf16[256,2048]{1,0:T(8,128)(2,1)}, bf16[1024,2048]{1,0:T(8,128)(2,1)}, bf16[1024,2048]{1,0:T(8,128)(2,1)}) async-done(((bf16[768,2048]{1,0:T(8,128)(2,1)}, bf16[256,2048]{1,0:T(8,128)(2,1)}, bf16[1024,2048]{1,0:T(8,128)(2,1)}, bf16[1024,2048]{1,0:T(8,128)(2,1)}), (bf16[768,2048]{1,0:T(8,128)(2,1)}, bf16[256,2048]{1,0:T(8,128)(2,1)}, ...) | async-done | bytes 12582928 | tf_op jit(solution)/shard_map/psum | solution.py:242
  706.6 2.9 convert_element_type.255
  709.5 3.6 convert_element_type.252
  713.1 4.4 convert_element_type.257
  717.6 4.4 convert_element_type.259
  722.0 76.5 %reduce-scatter.5.cloned.1.call-done = bf16[128,2048]{1,0:T(8,128)(2,1)} async-done(((bf16[1024,2048]{1,0:T(8,128)(2,1)}), bf16[128,2048]{1,0:T(8,128)(2,1)}) %reduce-scatter.5.cloned.1.call-update) | async-done | bytes 524304 | tf_op jit(solution)/shard_map/reduce_scatter | solution.py:180
  798.5 1.4 convert_reduce_fusion.2
  799.9 90.2 %reduce-scatter.3.cloned.1.call-done = bf16[128,2048]{1,0:T(8,128)(2,1)} async-done(((bf16[1024,2048]{1,0:T(8,128)(2,1)}), bf16[128,2048]{1,0:T(8,128)(2,1)}) %reduce-scatter.3.cloned.1.call-update) | async-done | bytes 524304 | tf_op jit(solution)/shard_map/reduce_scatter | solution.py:153
  890.1 3.0 fusion.74
  (196 shorter events, 34.9 us)
Async XLA Ops:
  7.2 9.1 %copy-start.14 = (bf16[768,2048]{1,0:T(8,128)(2,1)S(1)}, bf16[768,2048]{1,0:T(8,128)(2,1)}, u32[]{:S(2)}) copy-start(bf16[768,2048]{1,0:T(8,128)(2,1)} %param.22) | copy-start | bytes 9437188
  7.2 149.9 %all-gather.5.cloned.1.call-start = ((), (), s32[]{:S(2)}) async-start(), calls=%async_computation.7 | async-start | bytes 4718592 | tf_op jit(solution)/shard_map/all_gather | solution.py:94
  10.4 19.3 %copy-start.44 = (s32[1,9]{1,0:T(1,128)S(1)}, s32[1,9]{1,0:T(1,128)}, u32[]{:S(2)}) copy-start(s32[1,9]{1,0:T(1,128)} %param.19) | copy-start | bytes 112
  10.4 19.5 %copy-start.43 = (s32[1,9]{1,0:T(1,128)S(1)}, s32[1,9]{1,0:T(1,128)}, u32[]{:S(2)}) copy-start(s32[1,9]{1,0:T(1,128)} %param.18) | copy-start | bytes 112
  10.4 20.0 %copy-start.35 = (bf16[2048]{0:T(1024)(128)(2,1)S(1)}, bf16[2048]{0:T(1024)(128)(2,1)}, u32[]{:S(2)}) copy-start(bf16[2048]{0:T(1024)(128)(2,1)} %param.26) | copy-start | bytes 12292
  10.4 20.6 %copy-start.36 = (bf16[2048]{0:T(1024)(128)(2,1)S(1)}, bf16[2048]{0:T(1024)(128)(2,1)}, u32[]{:S(2)}) copy-start(bf16[2048]{0:T(1024)(128)(2,1)} %param.20) | copy-start | bytes 12292
  10.4 20.6 %copy-start.37 = (bf16[2048]{0:T(1024)(128)(2,1)S(1)}, bf16[2048]{0:T(1024)(128)(2,1)}, u32[]{:S(2)}) copy-start(bf16[2048]{0:T(1024)(128)(2,1)} %param.27) | copy-start | bytes 12292
  10.4 21.2 %copy-start.38 = (bf16[2048]{0:T(1024)(128)(2,1)S(1)}, bf16[2048]{0:T(1024)(128)(2,1)}, u32[]{:S(2)}) copy-start(bf16[2048]{0:T(1024)(128)(2,1)} %param.21) | copy-start | bytes 12292
  10.4 143.7 %all-to-all-start = ((bf16[256,8,256]{0,2,1:T(8,128)(2,1)}), bf16[256,8,256]{0,2,1:T(8,128)(2,1)}, u32[]{:S(2)}, u32[]{:S(2)}) async-start(bf16[256,8,256]{0,2,1:T(8,128)(2,1)} %bitcast.17), calls=%async_computation | async-start | bytes 2097152 | tf_op jit(solution)/shard_map/all_to_all | solution.py:106
  16.2 210.4 %all-gather.7.cloned.1.call-start = ((), (), s32[]{:S(2)}) async-start(), calls=%async_computation.8 | async-start | bytes 4718592 | tf_op jit(solution)/shard_map/all_gather | solution.py:95
  18.0 130.7 %collective-permute-start = (bf16[256,2048]{1,0:T(8,128)(2,1)}, bf16[256,2048]{1,0:T(8,128)(2,1)S(1)}, u32[]{:S(2)}, u32[]{:S(2)}) collective-permute-start(bf16[256,2048]{1,0:T(8,128)(2,1)} %get-tuple-element.36), channel_id=1, source_target_pairs={{0,0},{1,3},{2,6},{3,1},{4,4},{5,7},{6,2},{7,5},{8,8},{9,11},{10,1... | collective-permute-start | bytes 3145736 | tf_op jit(solution)/shard_map/ppermute | solution.py:100
  20.1 128.5 %collective-permute-start.2 = (bf16[256,2048]{1,0:T(8,128)(2,1)}, bf16[256,2048]{1,0:T(8,128)(2,1)}, u32[]{:S(2)}, u32[]{:S(2)}) collective-permute-start(bf16[256,2048]{1,0:T(8,128)(2,1)} %get-tuple-element.37), channel_id=1, source_target_pairs={{0,2},{1,5},{2,0},{3,3},{4,6},{5,1},{6,4},{7,7},{8,10},{9,13},{10,... | collective-permute-start | bytes 3145736 | tf_op jit(solution)/shard_map/ppermute | solution.py:100
  29.6 122.2 %collective-permute-start.1 = (bf16[256,2048]{1,0:T(8,128)(2,1)}, bf16[256,2048]{1,0:T(8,128)(2,1)}, u32[]{:S(2)}, u32[]{:S(2)}) collective-permute-start(bf16[256,2048]{1,0:T(8,128)(2,1)} %get-tuple-element.38), channel_id=1, source_target_pairs={{0,1},{1,4},{2,7},{3,2},{4,5},{5,0},{6,3},{7,6},{8,9},{9,12},{10,1... | collective-permute-start | bytes 3145736 | tf_op jit(solution)/shard_map/ppermute | solution.py:100
  34.9 6.2 copy-start.6
  148.7 3.2 copy-start.23
  154.1 109.5 %copy-start.3 = (bf16[3,256,2048]{2,1,0:T(8,128)(2,1)}, bf16[3,256,2048]{2,1,0:T(8,128)(2,1)S(1)}, u32[]{:S(2)}) copy-start(bf16[3,256,2048]{2,1,0:T(8,128)(2,1)S(1)} %pad_maximum_fusion) | copy-start | bytes 9437188
  157.1 3.4 copy-start
  163.9 3.1 copy-start.11
  165.2 1.7 copy-start.26
  168.2 1.1 copy-start.25
  179.6 7.5 copy-start.42
  183.2 3.9 copy-start.12
  226.7 5.0 copy-start.4
  231.6 2.4 copy-start.49
  236.0 2.5 copy-start.18
  236.0 2.5 copy-start.20
  238.5 1.4 copy-start.17
  238.5 1.3 copy-start.19
  242.1 1.2 copy-start.16
  247.6 4.6 copy-start.21
  258.8 4.7 copy-start.22
  263.6 5.5 copy-start.1
  263.6 5.5 copy-start.33
  263.6 5.5 copy-start.34
  263.6 5.5 copy-start.41
  263.6 6.3 copy-start.45
  269.9 14.9 %copy-start.46 = (bf16[1024,2048]{1,0:T(8,128)(2,1)S(1)}, bf16[1024,2048]{1,0:T(8,128)(2,1)}, u32[]{:S(2)}) copy-start(bf16[1024,2048]{1,0:T(8,128)(2,1)} %param.30) | copy-start | bytes 12582916
  269.9 14.9 %copy-start.47 = (bf16[1,1024,2048]{2,1,0:T(8,128)(2,1)S(1)}, bf16[1,1024,2048]{2,1,0:T(8,128)(2,1)}, u32[]{:S(2)}) copy-start(bf16[1,1024,2048]{2,1,0:T(8,128)(2,1)} %all-gather.7.cloned.1.call-done) | copy-start | bytes 12582916
  290.9 6.9 copy-start.51
  291.0 6.9 copy-start.28
  297.9 8.1 copy-start.27
  300.3 9.3 %copy-start.24 = (bf16[1,256,2048]{2,1,0:T(8,128)(2,1)S(1)}, bf16[1,256,2048]{2,1,0:T(8,128)(2,1)}, u32[]{:S(2)}) copy-start(bf16[1,256,2048]{2,1,0:T(8,128)(2,1)} %fusion.51) | copy-start | bytes 3145732
  300.3 76.2 %all-to-all-start.1 = ((bf16[8,256,256]{1,2,0:T(8,128)(2,1)}), bf16[8,256,256]{1,2,0:T(8,128)(2,1)S(1)}, u32[]{:S(2)}, u32[]{:S(2)}) async-start(bf16[8,256,256]{1,2,0:T(8,128)(2,1)} %bitcast.171), calls=%async_computation.3 | async-start | bytes 2097152 | tf_op jit(solution)/shard_map/all_to_all | solution.py:234
  306.0 174.5 %all-reduce.4.cloned.1.call-start = ((), (), s32[]{:S(2)}) async-start(), calls=%async_computation.6 | async-start | bytes 196608 | tf_op jit(solution)/shard_map/psum | solution.py:217
  306.0 21.1 %slice-start = ((s8[8388608]{0:T(1024)(128)(4,1)}), s8[4194304]{0:T(1024)(128)(4,1)S(1)}, s32[]{:S(2)}) async-start(s8[8388608]{0:T(1024)(128)(4,1)} %bitcast.172), calls=%async_computation.10 | async-start | bytes 8388608
  309.6 17.5 %slice-start.1 = ((s8[8388608]{0:T(1024)(128)(4,1)}), s8[4194304]{0:T(1024)(128)(4,1)S(1)}, s32[]{:S(2)}) async-start(s8[8388608]{0:T(1024)(128)(4,1)} %bitcast.172), calls=%async_computation.11 | async-start | bytes 8388608
  311.3 15.8 %copy-start.2 = (bf16[1,1024,2048]{2,1,0:T(8,128)(2,1)S(1)}, bf16[1,1024,2048]{2,1,0:T(8,128)(2,1)}, u32[]{:S(2)}) copy-start(bf16[1,1024,2048]{2,1,0:T(8,128)(2,1)} %all-gather.5.cloned.1.call-done) | copy-start | bytes 12582916
  313.2 50.5 %collective-permute-start.3 = (bf16[256,2048]{1,0:T(8,128)(2,1)}, bf16[256,2048]{1,0:T(8,128)(2,1)}, u32[]{:S(2)}, u32[]{:S(2)}) collective-permute-start(bf16[256,2048]{1,0:T(8,128)(2,1)} %get-tuple-element.33), channel_id=1, source_target_pairs={{0,0},{3,1},{6,2},{1,3},{4,4},{7,5},{2,6},{5,7},{8,8},{11,9},{14,1... | collective-permute-start | bytes 3145736 | tf_op jit(solution)/shard_map/ppermute | solution.py:231
  315.5 48.2 %collective-permute-start.5 = (bf16[256,2048]{1,0:T(8,128)(2,1)}, bf16[256,2048]{1,0:T(8,128)(2,1)}, u32[]{:S(2)}, u32[]{:S(2)}) collective-permute-start(bf16[256,2048]{1,0:T(8,128)(2,1)} %get-tuple-element.34), channel_id=1, source_target_pairs={{2,0},{5,1},{0,2},{3,3},{6,4},{1,5},{4,6},{7,7},{10,8},{13,9},{8,1... | collective-permute-start | bytes 3145736 | tf_op jit(solution)/shard_map/ppermute | solution.py:231
  324.9 12.7 %copy-start.31 = (f32[2048]{0:T(1024)S(1)}, f32[2048]{0:T(1024)}, u32[]{:S(2)}) copy-start(f32[2048]{0:T(1024)} %convert_reduce_fusion.3) | copy-start | bytes 24580
  324.9 48.4 %collective-permute-start.4 = (bf16[256,2048]{1,0:T(8,128)(2,1)}, bf16[256,2048]{1,0:T(8,128)(2,1)}, u32[]{:S(2)}, u32[]{:S(2)}) collective-permute-start(bf16[256,2048]{1,0:T(8,128)(2,1)} %get-tuple-element.35), channel_id=1, source_target_pairs={{1,0},{4,1},{7,2},{2,3},{5,4},{0,5},{3,6},{6,7},{9,8},{12,9},{15,1... | collective-permute-start | bytes 3145736 | tf_op jit(solution)/shard_map/ppermute | solution.py:231
  338.3 368.2 %all-reduce.6.cloned.1.call-start = ((), (), s32[]{:S(2)}) async-start(), calls=%async_computation.9 | async-start | bytes 25165824 | tf_op jit(solution)/shard_map/psum | solution.py:242
  338.4 10.1 %copy-start.48 = (bf16[1,1024,2048]{2,1,0:T(8,128)(2,1)S(1)}, bf16[1,1024,2048]{2,1,0:T(8,128)(2,1)}, u32[]{:S(2)}) copy-start(bf16[1,1024,2048]{2,1,0:T(8,128)(2,1)} %all-gather.7.cloned.1.call-done) | copy-start | bytes 12582916
  338.4 10.1 %copy-start.50 = (bf16[1024,1024]{1,0:T(8,128)(2,1)S(1)}, bf16[1024,1024]{1,0:T(8,128)(2,1)}, u32[]{:S(2)}) copy-start(bf16[1024,1024]{1,0:T(8,128)(2,1)} %get-tuple-element.68) | copy-start | bytes 6291460
  377.9 420.5 %reduce-scatter.5.cloned.1.call-start = ((), (), s32[]{:S(2)}) async-start(), calls=%async_computation.5 | async-start | bytes 4718592 | tf_op jit(solution)/shard_map/reduce_scatter | solution.py:180
  378.5 7.1 copy-start.13
  378.5 7.1 copy-start.29
  378.5 511.5 %reduce-scatter.3.cloned.1.call-start = ((), (), s32[]{:S(2)}) async-start(), calls=%async_computation.4 | async-start | bytes 4718592 | tf_op jit(solution)/shard_map/reduce_scatter | solution.py:153
  481.8 411.3 %copy-start.32 = (f32[2048]{0:T(1024)}, f32[2048]{0:T(1024)S(1)}, u32[]{:S(2)}) copy-start(f32[2048]{0:T(1024)S(1)} %get-tuple-element.103) | copy-start | bytes 24580
  706.6 2.9 copy-start.15
  709.5 3.6 copy-start.10
  713.1 4.5 copy-start.9
  717.5 80.9 %copy-start.8 = (bf16[1,128,2048]{2,1,0:T(8,128)(2,1)S(1)}, bf16[1,128,2048]{2,1,0:T(8,128)(2,1)}, u32[]{:S(2)}) copy-start(bf16[1,128,2048]{2,1,0:T(8,128)(2,1)} %param.16) | copy-start | bytes 1572868
  717.5 172.5 %copy-start.7 = (bf16[1,128,2048]{2,1,0:T(8,128)(2,1)S(1)}, bf16[1,128,2048]{2,1,0:T(8,128)(2,1)}, u32[]{:S(2)}) copy-start(bf16[1,128,2048]{2,1,0:T(8,128)(2,1)} %param.17) | copy-start | bytes 1572868
  (4 other events, 3.1 us)
Sparse Core Ops, SparseCore 0:
  10.1 142.9 all-gather.4
  155.3 71.3 all-gather.6
  338.5 141.9 all-reduce.3
  484.2 222.3 all-reduce.5
  710.1 88.3 reduce-scatter.4
  802.4 87.6 reduce-scatter.2

commit v2 on v1

--- a/solution.py
+++ b/solution.py
@@ -1,8 +1,11 @@
+import functools
 import math
 
 import jax
 import jax.numpy as jnp
 from jax import lax
+from jax.experimental import pallas as pl
+from jax.experimental.pallas import tpu as pltpu
 from jax.sharding import PartitionSpec as P
 
 D = 2048
@@ -62,6 +65,389 @@
 
 def dot_tn(a, b):
     return lax.dot_general(a, b, (((0,), (0,)), ((), ())), preferred_element_type=f32)
+
+
+MESH = pl.DeviceIdType.MESH
+RAILS = 2
+
+
+def place(group):
+    dp = lax.axis_index("dp")
+    ctx = lax.axis_index("ctx")
+    return dp, ctx, ctx // RAILS, ctx % RAILS, group // RAILS
+
+
+def copy_to(src, dst, send, recv, device):
+    return pltpu.make_async_remote_copy(
+        src_ref=src,
+        dst_ref=dst,
+        send_sem=send,
+        recv_sem=recv,
+        device_id=device,
+        device_id_type=MESH,
+    )
+
+
+def signal(device):
+    barrier = pltpu.get_barrier_semaphore()
+    pl.semaphore_signal(barrier, inc=1, device_id=device, device_id_type=MESH)
+
+
+def arrive(count):
+    pl.semaphore_wait(pltpu.get_barrier_semaphore(), count)
+
+
+def gather_kernel(group, *refs):
+    count = 2
+    sources, outs = refs[:count], refs[count : 2 * count]
+    own_sem, y_send, y_recv, up_send, up_recv, down_send, down_recv = refs[2 * count :]
+    dp, ctx, z, y, depth = place(group)
+    rows = sources[0].shape[0]
+    other = (dp, z * RAILS + 1 - y)
+    above = (dp, jnp.minimum(z + 1, depth - 1) * RAILS + y)
+    below = (dp, jnp.maximum(z - 1, 0) * RAILS + y)
+    has_above, has_below = z < depth - 1, z > 0
+
+    signal(other)
+    pl.when(has_above)(lambda: signal(above))
+    pl.when(has_below)(lambda: signal(below))
+    arrive(1 + has_above.astype(jnp.int32) + has_below.astype(jnp.int32))
+
+    def chunk(i, at_z, at_y):
+        start = pl.multiple_of((at_z * RAILS + at_y) * rows, rows)
+        return outs[i].at[pl.ds(start, rows)]
+
+    def to_other(i, at_z, source=None):
+        here = chunk(i, at_z, y)
+        return copy_to(
+            here if source is None else source, here, y_send.at[i, at_z], y_recv.at[i, at_z], other
+        )
+
+    def upward(i, k, source=None):
+        here = chunk(i, jnp.maximum(z - k, 0), y)
+        return copy_to(
+            here if source is None else source, here, up_send.at[i, k], up_recv.at[i, k + 1], above
+        )
+
+    def downward(i, k, source=None):
+        here = chunk(i, jnp.minimum(z + k, depth - 1), y)
+        return copy_to(
+            here if source is None else source,
+            here,
+            down_send.at[i, k],
+            down_recv.at[i, k + 1],
+            below,
+        )
+
+    own = [
+        pltpu.make_async_copy(sources[i], chunk(i, z, y), own_sem.at[i]) for i in range(count)
+    ]
+    for i in range(count):
+        to_other(i, z, sources[i]).start()
+        pl.when(has_above)(lambda i=i: upward(i, 0, sources[i]).start())
+        pl.when(has_below)(lambda i=i: downward(i, 0, sources[i]).start())
+        own[i].start()
+    for i in range(count):
+        for k in range(1, depth):
+
+            @pl.when(z >= k)
+            def _():
+                at_z = jnp.maximum(z - k, 0)
+                here = chunk(i, at_z, y)
+                copy_to(here, here, up_send.at[i, 0], up_recv.at[i, k], above).wait_recv()
+                pl.when(has_above)(lambda: upward(i, k).start())
+                to_other(i, at_z).start()
+
+            @pl.when(z + k < depth)
+            def _():
+                at_z = jnp.minimum(z + k, depth - 1)
+                here = chunk(i, at_z, y)
+                copy_to(here, here, down_send.at[i, 0], down_recv.at[i, k], below).wait_recv()
+                pl.when(has_below)(lambda: downward(i, k).start())
+                to_other(i, at_z).start()
+
+    for i in range(count):
+        own[i].wait()
+        for k in range(depth - 1):
+            pl.when(has_above & (z >= k))(lambda: upward(i, k).wait_send())
+            pl.when(has_below & (z + k < depth))(lambda: downward(i, k).wait_send())
+        for at_z in range(depth):
+            to_other(i, at_z).wait_send()
+            here = chunk(i, at_z, 1 - y)
+            copy_to(here, here, y_send.at[i, at_z], y_recv.at[i, at_z], other).wait_recv()
+
+
+def gather_tokens(group, first, second):
+    rows, columns = first.shape
+    depth = group // RAILS
+    sems = pltpu.SemaphoreType.DMA
+    out = jax.ShapeDtypeStruct((group * rows, columns), first.dtype)
+    return pl.pallas_call(
+        functools.partial(gather_kernel, group),
+        out_shape=(out, out),
+        in_specs=[pl.BlockSpec(memory_space=pl.ANY)] * 2,
+        out_specs=[pl.BlockSpec(memory_space=pl.ANY)] * 2,
+        scratch_shapes=[sems((2,))] + [sems((2, depth))] * 6,
+        compiler_params=pltpu.CompilerParams(collective_id=0, has_side_effects=True),
+        name="gather_tokens",
+    )(first, second)
+
+
+def reduce_kernel(group, tiles, *refs):
+    count = len(tiles)
+    parts, grads, vectors = refs[:2], refs[2 : 2 + count], refs[2 + count]
+    refs = refs[3 + count :]
+    outs, grads_out, vectors_out = refs[:2], refs[2 : 2 + count], refs[2 + count]
+    refs = refs[3 + count :]
+    own, y_buf, up_buf, down_buf, mine, from_core, from_x, vec_buf = refs[:8]
+    (
+        own_sem,
+        y_send,
+        y_recv,
+        up_send,
+        up_recv,
+        down_send,
+        down_recv,
+        out_sem,
+        mine_sem,
+        core_send,
+        core_recv,
+        x_send,
+        x_recv,
+        keep_sem,
+        done_send,
+        done_recv,
+        vec_send,
+        vec_recv,
+    ) = refs[8:]
+    dp, ctx, z, y, depth = place(group)
+    rows = outs[0].shape[0]
+    x, core = dp // 2, dp % 2
+    other = (dp, z * RAILS + 1 - y)
+    above = (dp, jnp.minimum(z + 1, depth - 1) * RAILS + y)
+    below = (dp, jnp.maximum(z - 1, 0) * RAILS + y)
+    sibling = (x * 2 + 1 - core, ctx)
+    across = ((1 - x) * 2 + core, ctx)
+    pair = (dp, (z + 1 - 2 * (z % 2)) * RAILS + y)
+    pair_far = (dp, lax.rem(z + 2, depth) * RAILS + y)
+    has_above, has_below = z < depth - 1, z > 0
+
+    for device in (other, sibling, across, pair, pair_far):
+        signal(device)
+    inner = (z > 0) & (z < depth - 1)
+    pl.when(inner)(lambda: signal((dp, jnp.clip(z - 1 + 2 * (z % 2), 0, depth - 1) * RAILS + y)))
+    arrive(5 + inner.astype(jnp.int32))
+
+    def part_chunk(i, at_z, at_y):
+        start = pl.multiple_of((at_z * RAILS + at_y) * rows, rows)
+        return parts[i].at[pl.ds(start, rows)]
+
+    half = mine.shape[1]
+
+    spots = [(n, m) for n, amount in enumerate(tiles) for m in range(amount)]
+    tiles = len(spots)
+
+    def tile_half(arrays, t, which):
+        n, m = spots[t]
+        start = pl.multiple_of((2 * m + which) * half, half)
+        return arrays[n].at[pl.ds(start, half)]
+
+    def fetch(t):
+        return pltpu.make_async_copy(tile_half(grads, t, core), mine.at[t], mine_sem.at[t])
+
+    def to_core(t):
+        return copy_to(
+            tile_half(grads, t, 1 - core),
+            from_core.at[t],
+            core_send.at[t],
+            core_recv.at[t],
+            sibling,
+        )
+
+    def to_x(t):
+        return copy_to(mine.at[t], from_x.at[t], x_send.at[t], x_recv.at[t], across)
+
+    def keep(t):
+        return pltpu.make_async_copy(
+            from_core.at[t], tile_half(grads_out, t, core), keep_sem.at[t]
+        )
+
+    def finish(t):
+        return copy_to(
+            from_core.at[t],
+            tile_half(grads_out, t, core),
+            done_send.at[t],
+            done_recv.at[t],
+            sibling,
+        )
+
+    def add(target, left, right):
+        step = 32
+
+        @pl.loop(0, target.shape[0] // step)
+        def _(n):
+            at = pl.ds(pl.multiple_of(n * step, step), step)
+            target[at, :] = (left[at, :].astype(f32) + right[at, :].astype(f32)).astype(
+                target.dtype
+            )
+
+    def core_sum(t):
+        fetch(t).wait()
+        to_core(t).wait_recv()
+        add(mine.at[t], mine.at[t], from_core.at[t])
+        to_x(t).start()
+
+    def x_sum(t):
+        to_x(t).wait_recv()
+        add(from_core.at[t], mine.at[t], from_x.at[t])
+        keep(t).start()
+        finish(t).start()
+
+    low = z < depth // 2
+    order = [
+        jnp.where(low, depth - 1, 0),
+        jnp.where(low, depth - 2, 1),
+        jnp.where(low, 1 - z, 2 * depth - 3 - z),
+        z,
+    ]
+
+    def hold(i, s):
+        return pltpu.make_async_copy(
+            part_chunk(i, order[s], y), own.at[i, order[s]], own_sem.at[i, s]
+        )
+
+    def swap(i, s):
+        return copy_to(
+            part_chunk(i, order[s], 1 - y),
+            y_buf.at[i, order[s]],
+            y_send.at[i, s],
+            y_recv.at[i, s],
+            other,
+        )
+
+    def upward(i, at):
+        return copy_to(own.at[i, at], up_buf.at[i, at], up_send.at[i, at], up_recv.at[i, at], above)
+
+    def downward(i, at):
+        return copy_to(
+            own.at[i, at], down_buf.at[i, at], down_send.at[i, at], down_recv.at[i, at], below
+        )
+
+    def scatter_step(i, s):
+        at = order[s]
+        hold(i, s).wait()
+        swap(i, s).wait_recv()
+        add(own.at[i, at], own.at[i, at], y_buf.at[i, at])
+
+        @pl.when((at >= z) & has_below)
+        def _():
+            upward(i, at).wait_recv()
+            add(own.at[i, at], own.at[i, at], up_buf.at[i, at])
+
+        @pl.when((at <= z) & has_above)
+        def _():
+            downward(i, at).wait_recv()
+            add(own.at[i, at], own.at[i, at], down_buf.at[i, at])
+
+        pl.when(at > z)(lambda: upward(i, at).start())
+        pl.when(at < z)(lambda: downward(i, at).start())
+
+    def scatter_out(i):
+        return pltpu.make_async_copy(own.at[i, z], outs[i], out_sem.at[i])
+
+    stages = (sibling, across, other, pair, pair_far)
+
+    def exchange(n):
+        return copy_to(
+            vec_buf.at[2 * n], vec_buf.at[2 * n + 1], vec_send.at[n], vec_recv.at[n], stages[n]
+        )
+
+    for t in range(tiles):
+        fetch(t).start()
+        to_core(t).start()
+    vec_buf[0] = vectors[...]
+    exchange(0).start()
+    for i in range(2):
+        for s in range(depth):
+            hold(i, s).start()
+            swap(i, s).start()
+    core_sum(0)
+    core_sum(1)
+    steps = [(i, s) for i in range(2) for s in range(depth)]
+    for t in range(tiles):
+        if t + 2 < tiles:
+            core_sum(t + 2)
+        if t < len(stages):
+            exchange(t).wait_recv()
+            total = vec_buf[2 * t] + vec_buf[2 * t + 1]
+            if t + 1 < len(stages):
+                vec_buf[2 * t + 2] = total
+                exchange(t + 1).start()
+            else:
+                vectors_out[...] = total
+        if t < len(steps):
+            scatter_step(*steps[t])
+            if steps[t][1] == depth - 1:
+                scatter_out(steps[t][0]).start()
+        x_sum(t)
+    for t in range(tiles):
+        to_core(t).wait_send()
+        to_x(t).wait_send()
+        keep(t).wait()
+        finish(t).wait_send()
+        copy_to(
+            from_core.at[t],
+            tile_half(grads_out, t, 1 - core),
+            done_send.at[t],
+            done_recv.at[t],
+            sibling,
+        ).wait_recv()
+    for n in range(len(stages)):
+        exchange(n).wait_send()
+    for i in range(2):
+        scatter_out(i).wait()
+        for s in range(depth):
+            swap(i, s).wait_send()
+            at = order[s]
+            pl.when(at > z)(lambda: upward(i, at).wait_send())
+            pl.when(at < z)(lambda: downward(i, at).wait_send())
+
+
+def reduce_all(group, first, second, grads, vectors):
+    tokens, columns = first.shape
+    depth = group // RAILS
+    rows = tokens // group
+    half = 128
+    tiles = [grad.shape[0] // (2 * half) for grad in grads]
+    sems = pltpu.SemaphoreType.DMA
+    part = jax.ShapeDtypeStruct((rows, columns), first.dtype)
+    anywhere = pl.BlockSpec(memory_space=pl.ANY)
+    vmem = pl.BlockSpec(memory_space=pltpu.VMEM)
+    chunks = pltpu.VMEM((2, depth, rows, columns), first.dtype)
+    halves = pltpu.VMEM((sum(tiles), half, columns), first.dtype)
+    results = pl.pallas_call(
+        functools.partial(reduce_kernel, group, tiles),
+        out_shape=(
+            part,
+            part,
+            *[jax.ShapeDtypeStruct(grad.shape, grad.dtype) for grad in grads],
+            jax.ShapeDtypeStruct(vectors.shape, vectors.dtype),
+        ),
+        in_specs=[anywhere] * (2 + len(grads)) + [vmem],
+        out_specs=[anywhere] * (2 + len(grads)) + [vmem],
+        scratch_shapes=[chunks] * 4
+        + [halves] * 3
+        + [pltpu.VMEM((10,) + vectors.shape, vectors.dtype)]
+        + [sems((2, depth))] * 7
+        + [sems((2,))]
+        + [sems((sum(tiles),))] * 8
+        + [sems((5,))] * 2,
+        compiler_params=pltpu.CompilerParams(
+            collective_id=1, has_side_effects=True, vmem_limit_bytes=56 * 2**20
+        ),
+        name="reduce_all",
+    )(first, second, *grads, vectors)
+    return results[0], results[1], results[2:-1], results[-1]
 
 
 def body(
@@ -91,18 +477,8 @@
     head_shape = (tokens, head_count, HEAD_DIM)
     scale = 1.0 / math.sqrt(HEAD_DIM)
 
-    hidden_all = lax.all_gather(hidden_in[0], "ctx", axis=0, tiled=True)
-    grad_all = lax.all_gather(grad_out[0], "ctx", axis=0, tiled=True)
-
-    blocks = w_qkv.reshape(3, head_cols, D)
-    arrived = jnp.stack(
-        [
-            lax.ppermute(blocks[j], "ctx", [(c, (3 * c + j) % group) for c in range(group)])
-            for j in range(3)
-        ]
-    )
-    slots = [(kind * group + me) % 3 for kind in range(3)]
-    w_heads = [lax.dynamic_index_in_dim(arrived, slot, 0, keepdims=False) for slot in slots]
+    hidden_all, grad_all = gather_tokens(group, hidden_in[0], grad_out[0])
+
     w_out_cols = lax.all_to_all(
         w_out, "ctx", split_axis=1, concat_axis=0, tiled=True
     )
@@ -127,16 +503,23 @@
     x_attn = (normed * gain_a + shift_attn.astype(f32)).astype(bf16)
     x_mlp = (normed * gain_m + shift_mlp.astype(f32)).astype(bf16)
 
-    my_bias = [
-        lax.dynamic_slice_in_dim(bias_qkv, kind * D + me * head_cols, head_cols).astype(f32)
+    my_bias = lax.dynamic_slice_in_dim(bias_qkv, me * 3 * head_cols, 3 * head_cols)
+    raw = dot_nt(x_attn, w_qkv) + my_bias.astype(f32)
+    arrived = []
+    for j in range(3):
+        turns = (3 * me + j) // group < 2
+        block = raw[:, j * head_cols : (j + 1) * head_cols].reshape(head_shape)
+        block = rotate(block, jnp.where(turns, cosine, 1.0), jnp.where(turns, sine, 0.0))
+        arrived.append(
+            lax.ppermute(
+                block.astype(bf16), "ctx", [(c, (3 * c + j) % group) for c in range(group)]
+            )
+        )
+    arrived = jnp.stack(arrived)
+    q, k, v = [
+        lax.dynamic_index_in_dim(arrived, (kind * group + me) % 3, 0, keepdims=False)
         for kind in range(3)
     ]
-    q_raw, k_raw, v_raw = [
-        (dot_nt(x_attn, w_heads[kind]) + my_bias[kind]).reshape(head_shape) for kind in range(3)
-    ]
-    q = rotate(q_raw, cosine, sine).astype(bf16)
-    k = rotate(k_raw, cosine, sine).astype(bf16)
-    v = v_raw.astype(bf16)
     scores = jnp.einsum("qhd,khd->hqk", q, k, preferred_element_type=f32) * scale
     scores = jnp.where(allowed[None], scores, masked_score)
     top = jnp.max(scores, axis=-1, keepdims=True)
@@ -149,11 +532,7 @@
     up_bias = lax.dynamic_slice_in_dim(bias_up, me * w_up.shape[0], w_up.shape[0]).astype(f32)
     pre_act = dot_nt(x_mlp, w_up) + up_bias
     act = jax.nn.gelu(pre_act, approximate=False).astype(bf16)
-    partial = dot_nt(attended, w_out_cols) + dot_nn(act, w_down)
-    summed = lax.psum_scatter(partial.astype(bf16), "ctx", scatter_dimension=0, tiled=True)
-    hidden_out = (
-        hidden_in[0].astype(f32) + summed.astype(f32) + bias_out.astype(f32) + bias_down.astype(f32)
-    ).astype(bf16)
+    partial = (dot_nt(attended, w_out_cols) + dot_nn(act, w_down)).astype(bf16)
 
     grad_w_down = dot_tn(act, grad_all).astype(bf16)
     pre_grad = (dot_nt(grad_all, w_down) * gelu_slope(pre_act)).astype(bf16)
@@ -173,17 +552,57 @@
         rotate(k_grad, cosine, -sine).astype(bf16).reshape(tokens, head_cols),
         v_grad.astype(bf16).reshape(tokens, head_cols),
     ]
-    attn_in_grad = sum(dot_nn(qkv_grad[kind], w_heads[kind]) for kind in range(3))
-    grad_heads = jnp.stack([dot_tn(qkv_grad[kind], x_attn).astype(bf16) for kind in range(3)])
-
-    back = attn_in_grad * gain_a + mlp_in_grad * gain_m
-    w_sum = lax.psum_scatter(back.astype(bf16), "ctx", scatter_dimension=0, tiled=True).astype(f32)
+    qkv_grad = jnp.stack(qkv_grad)
+    returned = []
+    for j in range(3):
+        kind_of_slot = sum(
+            kind * ((kind * group + me) % 3 == j).astype(jnp.int32) for kind in range(3)
+        )
+        block = lax.dynamic_index_in_dim(qkv_grad, kind_of_slot, 0, keepdims=False)
+        returned.append(
+            lax.ppermute(block, "ctx", [((3 * c + j) % group, c) for c in range(group)])
+        )
+    qkv_grad = jnp.concatenate(returned, axis=1)
+    attn_in_grad = dot_nn(qkv_grad, w_qkv)
+    grad_w_qkv = dot_tn(qkv_grad, x_attn).astype(bf16)
+    grad_w_out = lax.all_to_all(
+        grad_w_out_cols, "ctx", split_axis=0, concat_axis=1, tiled=True
+    )
+    back = (attn_in_grad * gain_a + mlp_in_grad * gain_m).astype(bf16)
+
+    def widen(part, length):
+        at = me * part.shape[0]
+        return lax.dynamic_update_slice(jnp.zeros((length,), f32), part, (at,))
+
+    grad_f = grad_out[0].astype(f32)
+    vectors = jnp.concatenate(
+        [
+            jnp.sum(attn_in_grad * normed, axis=0),
+            jnp.sum(attn_in_grad, axis=0),
+            jnp.sum(mlp_in_grad * normed, axis=0),
+            jnp.sum(mlp_in_grad, axis=0),
+            widen(jnp.sum(qkv_grad, axis=0, dtype=f32), 3 * D),
+            jnp.sum(grad_f, axis=0),
+            widen(jnp.sum(pre_grad, axis=0, dtype=f32), FF),
+        ]
+    )
+    summed, w_sum, sums, vectors = reduce_all(
+        group,
+        partial,
+        back,
+        (grad_w_down, grad_w_up, grad_w_out, grad_w_qkv),
+        vectors.reshape(-1, 1024),
+    )
+    vectors = vectors.reshape(-1)
+    w_sum = w_sum.astype(f32)
+    hidden_out = (
+        hidden_in[0].astype(f32) + summed.astype(f32) + bias_out.astype(f32) + bias_down.astype(f32)
+    ).astype(bf16)
     start = me * local_rows
     my_rstd = lax.dynamic_slice_in_dim(rstd, start, local_rows)
     my_normed = (
         hidden_in[0].astype(f32) - lax.dynamic_slice_in_dim(mean, start, local_rows)
     ) * my_rstd
-    grad_f = grad_out[0].astype(f32)
     grad_in = (
         grad_f
         + (
@@ -194,60 +613,26 @@
         * my_rstd
     )
 
-    def widen(part, length, at):
-        return lax.dynamic_update_slice(jnp.zeros((length,), f32), part, (at,))
-
-    bias_qkv_grad = jnp.concatenate(
-        [
-            widen(jnp.sum(qkv_grad[kind], axis=0, dtype=f32), D, me * head_cols)
-            for kind in range(3)
-        ]
-    )
-    vectors = jnp.concatenate(
-        [
-            jnp.sum(attn_in_grad * normed, axis=0),
-            jnp.sum(attn_in_grad, axis=0),
-            jnp.sum(mlp_in_grad * normed, axis=0),
-            jnp.sum(mlp_in_grad, axis=0),
-            bias_qkv_grad,
-            jnp.sum(grad_f, axis=0),
-            widen(jnp.sum(pre_grad, axis=0, dtype=f32), FF, me * w_up.shape[0]),
-        ]
-    )
-    vectors = lax.psum(vectors, ("dp", "ctx"))
     cuts = [D, D, D, D, 3 * D, D, FF]
     ends = [sum(cuts[: i + 1]) for i in range(len(cuts))]
     gain_grad_a, shift_grad_a, gain_grad_m, shift_grad_m, qkv_bias_grad, out_bias_grad, up_bias_grad = [
         vectors[end - cut : end] for cut, end in zip(cuts, ends)
     ]
 
-    returned = []
-    for j in range(3):
-        kind_of_slot = sum(
-            kind * ((kind * group + me) % 3 == j).astype(jnp.int32) for kind in range(3)
-        )
-        block = lax.dynamic_index_in_dim(grad_heads, kind_of_slot, 0, keepdims=False)
-        returned.append(
-            lax.ppermute(block, "ctx", [((3 * c + j) % group, c) for c in range(group)])
-        )
-    grad_w_qkv = jnp.concatenate(returned, axis=0)
-    grad_w_out = lax.all_to_all(
-        grad_w_out_cols, "ctx", split_axis=0, concat_axis=1, tiled=True
-    )
     return (
         hidden_out[None],
         grad_in[None],
         gain_grad_a,
         shift_grad_a,
-        lax.psum(grad_w_qkv, "dp").astype(f32),
+        sums[3].astype(f32),
         qkv_bias_grad,
-        lax.psum(grad_w_out, "dp").astype(f32),
+        sums[2].astype(f32),
         out_bias_grad,
         gain_grad_m,
         shift_grad_m,
-        lax.psum(grad_w_up, "dp").astype(f32),
+        sums[1].astype(f32),
         up_bias_grad,
-        lax.psum(grad_w_down, "dp").astype(f32),
+        sums[0].astype(f32),
         out_bias_grad,
     )
 

time: 910 us -> 510 us (0.56)
  waiting for transfers between devices: 632 us -> 12.3 us
  Pallas kernels: 0 us -> 289 us
  local copies, waits for them, and re-layouts: 45.1 us -> 25.1 us
  matrix products: 121 us -> 104 us
  between operations: 15.4 us -> 2.06 us
  starting transfers between devices: 37.3 us -> 27 us
    psum x2 -> x0, waiting for transfers between devices: 313 us -> none  [the longest x1 222 us: body(): lax.psum(grad_w_qkv, 'dp').astype(f32)]
    pallas_call x0 -> x2, Pallas kernels: none -> 289 us  [the longest x1 197 us: reduce_all(): pl.pallas_call(functools.partial(reduce_kernel, group, tiles), out_shape=...]
    reduce_scatter x2 -> x0, waiting for transfers between devices: 167 us -> none  [the longest x1 90.2 us: body(): lax.psum_scatter(partial.astype(bf16), 'ctx', scatter_dimension=0, tiled=...]
    ppermute x3, waiting for transfers between devices: 110 us -> 0.01 us  [body(): lax.ppermute(block.astype(bf16), 'ctx', [(c, (3 * c + j) % group) for c i...]
    all_gather x2 -> x0, waiting for transfers between devices: 23 us -> none  [the longest x1 23 us: body(): grad_all = lax.all_gather(grad_out[0], 'ctx', axis=0, tiled=True)]
    dot_general x6 -> x4, matrix products: 37.8 us -> 25.7 us  [dot_nn(): lax.dot_general(a, b, (((1,), (0,)), ((), ())), preferred_element_type=f32)]
    dot_general x6 -> x4, matrix products: 30.7 us -> 23.7 us  [dot_tn(): lax.dot_general(a, b, (((0,), (0,)), ((), ())), preferred_element_type=f32)]
    dot_general x6 -> x4, matrix products: 29 us -> 31.9 us  [dot_nt(): lax.dot_general(a, b, (((1,), (1,)), ((), ())), preferred_element_type=f32)]
  transfers between devices with their start and end apart: 14 -> 8, of which waited for: 9 -> 1; matrix products, arithmetic and copies ran while one was open for 15% -> 24% of each run, Pallas kernels for 0% -> 0%
where the time goes in v2:
time: 510 us; the launch traced here: 504 us
  Pallas kernels  289 us (57%)
  matrix products  104 us (20%)
  other arithmetic  43.3 us (8%)
  starting transfers between devices  27 us (5%)
  local copies, waits for them, and re-layouts  25.1 us (5%)
  waiting for transfers between devices  12.3 us (2%)
    pallas_call x1, Pallas kernels, reduce_all(): pl.pallas_call(functools.partial(reduce_kernel, group, tiles), out_shape=...  197 us
    pallas_call x1, Pallas kernels, gather_tokens(): pl.pallas_call(functools.partial(gather_kernel, group), out_shape=(out, o...  92.3 us
    dot_general x4, matrix products, dot_nt(): lax.dot_general(a, b, (((1,), (1,)), ((), ())), preferred_element_type=f32)  31.9 us
    dot_general x4, matrix products, dot_nn(): lax.dot_general(a, b, (((1,), (0,)), ((), ())), preferred_element_type=f32)  25.7 us
    dot_general x4, matrix products, dot_tn(): lax.dot_general(a, b, (((0,), (0,)), ((), ())), preferred_element_type=f32)  23.7 us
    ppermute x3, waiting for transfers between devices, body(): lax.ppermute(block, 'ctx', [((3 * c + j) % group, c) for c in range(group)])  12.3 us
    unnamed x104, local copies, waits for them, and re-layouts  10.8 us
  transfers between devices with their start and end apart: 8, of which 1 were waited for; matrix products, arithmetic and copies ran while one was open for 24% of the time, Pallas kernels for 0%

profile of v2, /device:TPU:13, one launch (start us, length us, event | category | flops | bytes accessed | tf_op | source)
XLA Modules:
  0.0 503.7 jit_solution(10831241681143316640)
XLA Ops:
  1.2 92.3 %gather_tokens.1 = (bf16[1024,2048]{1,0:T(8,128)(2,1)}, bf16[1024,2048]{1,0:T(8,128)(2,1)}) custom-call(bf16[128,2048]{1,0:T(8,128)(2,1)} %bitcast.148, bf16[128,2048]{1,0:T(8,128)(2,1)} %bitcast.149), custom_call_target="tpu_custom_call" | custom-call | tf_op jit(solution)/shard_map/gather_tokens/pallas_call | solution.py:185
  93.5 3.0 convert_reduce_fusion
  96.9 1.2 fusion.13
  98.2 0.8 dynamic-slice_convert_fusion.1
  99.0 5.8 %convolution_add_fusion = f32[1024,768]{0,1:T(8,128)S(1)} fusion(bf16[768,2048]{1,0:T(8,128)(2,1)S(1)} %copy-done, f32[768]{0:T(1024)S(1)} %dynamic-slice_convert_fusion.1, bf16[1024,2048]{1,0:T(8,128)(2,1)} %get-tuple-element.23, f32[2048]{0:T(1024)S(1)} %convert_element_type.169, f32[2048]{0:T(1024)S(1)} %convert_element_type.168, ...), kind=kOutput, calls=%fused_computation.65 | convolution fusion | flops 3234594816 | bytes 10513408 | tf_op jit(solution)/shard_map/dot_general | solution.py:59
  104.8 1.7 fusion.131
  106.5 0.8 slice_negate_fusion.4
  107.6 0.9 select_reduce_fusion.1
  108.6 0.8 select_reduce_fusion.2
  109.6 0.7 broadcast_multiply_fusion
  110.4 1.0 fusion.100
  111.4 1.1 fusion.98
  112.5 0.8 pad_maximum_fusion.2
  113.3 1.9 collective-permute-start
  115.2 1.0 slice_negate_fusion.3
  116.2 1.2 slice.230
  117.4 1.0 fusion.96
  118.5 0.8 pad_maximum_fusion.3
  119.3 1.2 collective-permute-start.1
  120.7 0.8 pad_maximum_fusion.4
  121.5 5.3 %collective-permute-start.2 = (bf16[1024,2,128]{0,2,1:T(8,128)(2,1)}, bf16[1024,2,128]{0,2,1:T(8,128)(2,1)}, u32[]{:S(2)}, u32[]{:S(2)}) collective-permute-start(bf16[1024,2,128]{0,2,1:T(8,128)(2,1)} %pad_maximum_fusion.4), channel_id=1, source_target_pairs={{0,2},{1,5},{2,0},{3,3},{4,6},{5,1},{6,4},{7,7},{8,10},{9,13},{10,... | collective-permute-start | bytes 1572872 | tf_op jit(solution)/shard_map/ppermute | solution.py:514
  126.8 2.3 copy.86
  129.1 7.3 %all-to-all-start = ((bf16[256,8,256]{0,2,1:T(8,128)(2,1)}), bf16[256,8,256]{0,2,1:T(8,128)(2,1)}, u32[]{:S(2)}, u32[]{:S(2)}) async-start(bf16[256,8,256]{0,2,1:T(8,128)(2,1)} %bitcast.153), calls=%async_computation | async-start | bytes 2097152 | tf_op jit(solution)/shard_map/all_to_all | solution.py:482
  136.5 0.7 dynamic-slice_convert_fusion
  137.2 16.6 %fusion.17 = (bf16[1024,1024]{1,0:T(8,128)(2,1)S(1)}, f32[1024,1024]{1,0:T(8,128)S(1)}) fusion(f32[1024]{0:T(1024)S(1)} %dynamic-slice_convert_fusion, bf16[1024,2048]{1,0:T(8,128)(2,1)} %param.28, bf16[1024,2048]{1,0:T(8,128)(2,1)} %get-tuple-element.23, f32[2048]{0:T(1024)S(1)} %convert_element_type.180, f32[2048]{0:T(1024)S(1)} %convert_element_type.179, ...), kind=kOutput, calls=%fused_computation.27 | convolution fusion | flops 4376756224 | bytes 14708736 | tf_op jit(solution)/shard_map/dot_general | solution.py:59
  153.9 6.1 %convert_reduce_fusion.1 = (f32[1024]{0:T(1024)S(1)}, bf16[1024,1024]{1,0:T(8,128)(2,1)S(1)}) fusion(f32[1024,1024]{1,0:T(8,128)S(1)} %get-tuple-element.77, f32[1024]{0:T(1024)S(1)} %dynamic-slice_convert_fusion, bf16[1024,2048]{1,0:T(8,128)(2,1)S(1)} %copy-done.35, bf16[1024,2048]{1,0:T(8,128)(2,1)S(1)} %copy-done.34), kind=kOutput, calls=%fused_computation.34 | convolution fusion | flops 4308597760 | bytes 14688256 | tf_op jit(solution)/shard_map/dot_general | solution.py:59
  160.0 6.7 %fusion.142 = f32[1024,2048]{1,0:T(8,128)} fusion(bf16[1024,1024]{1,0:T(8,128)(2,1)S(1)} %get-tuple-element.83, bf16[1024,2048]{1,0:T(8,128)(2,1)S(1)} %copy-done.33), kind=kOutput, calls=%fused_computation.223 | convolution fusion | flops 4294967296 | bytes 14680064 | tf_op jit(solution)/shard_map/dot_general | solution.py:63
  166.7 7.1 %convolution_convert_fusion.refs_3_ = bf16[1024,2048]{1,0:T(8,128)(2,1)} fusion(bf16[1024,1024]{1,0:T(8,128)(2,1)S(1)} %get-tuple-element.83, bf16[1024,2048]{1,0:T(8,128)(2,1)S(1)} %copy-done.2, f32[2048]{0:T(1024)S(1)} %convert_element_type.180, f32[2048]{0:T(1024)S(1)} %convert_element_type.179, f32[1024]{0:T(1024)S(1)} %copy-done.28, ...), kind=kOutput, calls=%fused_computation.56 | convolution fusion | flops 4309647360 | bytes 10510336 | tf_op jit(solution)/shard_map/dot_general | solution.py:67
  173.8 6.7 %fusion.141 = f32[1024,2048]{1,0:T(8,128)} fusion(bf16[1024,1024]{1,0:T(8,128)(2,1)S(1)} %get-tuple-element.76, bf16[1024,2048]{1,0:T(8,128)(2,1)S(1)} %copy-done.34), kind=kOutput, calls=%fused_computation.222 | convolution fusion | flops 4294967296 | bytes 14680064 | tf_op jit(solution)/shard_map/dot_general | solution.py:63
  180.5 6.3 %convolution_convert_fusion.1.refs_2_ = bf16[1024,2048]{1,0:T(8,128)(2,1)} fusion(bf16[1024,1024]{1,0:T(8,128)(2,1)S(1)} %get-tuple-element.76, bf16[1024,2048]{1,0:T(8,128)(2,1)S(1)} %copy-done.35), kind=kOutput, calls=%fused_computation.57 | convolution fusion | flops 4297064448 | bytes 10485760 | tf_op jit(solution)/shard_map/dot_general | solution.py:67
  187.0 2.1 fusion.32
  189.1 3.8 copy.82
  193.2 1.1 convert_reduce_fusion.4
  194.3 2.7 pad_maximum_fusion
  197.0 8.3 %fusion.132 = (f32[2,1024]{1,0:T(2,128)S(1)}, f32[2,1024,1024]{1,2,0:T(8,128)}) fusion(pred[1024,1024]{0,1:T(8,128)(4,1)} %copy.82, bf16[3,1024,2,128]{1,3,2,0:T(8,128)(2,1)} %pad_maximum_fusion, s32[]{:T(128)S(6)} %select_n.160, s32[]{:T(128)S(6)} %select_n.158), kind=kOutput, calls=%fused_computation.221 | convolution fusion | flops 545260544 | bytes 10493960 | tf_op jit(solution)/shard_map/sub | solution.py:526
  205.3 4.4 fusion.41
  209.8 0.8 copy-done.14
  210.6 2.4 convolution_convert_fusion.3
  212.9 5.7 %all-to-all-start.1 = ((bf16[8,256,256]{2,1,0:T(8,128)(2,1)}), bf16[8,256,256]{2,1,0:T(8,128)(2,1)}, u32[]{:S(2)}, u32[]{:S(2)}) async-start(bf16[8,256,256]{2,1,0:T(8,128)(2,1)} %bitcast.165), calls=%async_computation.1 | async-start | bytes 2097152 | tf_op jit(solution)/shard_map/all_to_all | solution.py:568
  218.6 2.3 copy.87
  220.9 3.9 convolution_convert_fusion.4
  224.8 4.5 multiply_reduce_fusion
  229.4 1.3 slice-done.3
  230.7 2.4 multiply_convert_fusion
  233.2 1.5 fusion.39
  234.7 0.7 fusion.40
  235.7 1.5 fusion.44
  237.8 2.6 collective-permute-start.3
  240.4 2.1 collective-permute-start.4
  242.5 0.8 collective-permute-start.5
  243.4 3.4 add_convert_fusion.1.refs_0_
  246.7 12.3 %collective-permute-done.3 = bf16[1024,256]{0,1:T(8,128)(2,1)S(1)} collective-permute-done((bf16[1024,256]{0,1:T(8,128)(2,1)S(1)}, bf16[1024,256]{0,1:T(8,128)(2,1)S(1)}, u32[]{:S(2)}, u32[]{:S(2)}) %collective-permute-start.3) | collective-permute-done | bytes 524320 | tf_op jit(solution)/shard_map/ppermute | solution.py:563
  259.3 8.4 %fusion.129 = (f32[2048]{0:T(1024)S(1)}, f32[2048]{0:T(1024)S(1)}, bf16[1024,2048]{1,0:T(8,128)(2,1)}, f32[2048]{0:T(1024)S(1)}, f32[2048]{0:T(1024)S(1)}) fusion(f32[1024,2048]{1,0:T(8,128)S(1)} %bitcast.183, f32[1024]{0:T(1024)S(1)} %copy-done.28, f32[1024]{0:T(1024)S(1)} %broadcast_multiply_fusion.1, bf16[1024,2048]{1,0:T(8,128)(2,1)S(1)} %copy-done.3, ...), kind=kOutput, calls=%fused_computation.218 | convolution fusion | flops 3248480256 | bytes 21553152 | tf_op jit(solution)/shard_map/dot_general | solution.py:63
  269.0 7.9 %convolution_convert_fusion.2.refs_5_ = bf16[768,2048]{1,0:T(8,128)(2,1)} fusion(bf16[1024,768]{0,1:T(8,128)(2,1)} %copy-done.11, bf16[1024,2048]{1,0:T(8,128)(2,1)} %get-tuple-element.23, f32[2048]{0:T(1024)S(1)} %copy-done.20, f32[2048]{0:T(1024)S(1)} %convert_element_type.168, f32[1024]{0:T(1024)S(1)} %copy-done.28, f32[1024]{0:T(1024)S(1)} %broadcast_multiply_fusion.1), kind=kOutput, calls=%fused_computation.58 | convolution fusion | flops 3235381248 | bytes 8937472 | tf_op jit(solution)/shard_map/dot_general | solution.py:67
  276.9 2.3 copy.108
  279.3 197.1 %reduce_all.1 = (bf16[128,2048]{1,0:T(8,128)(2,1)}, bf16[128,2048]{1,0:T(8,128)(2,1)}, bf16[1024,2048]{1,0:T(8,128)(2,1)}, bf16[1024,2048]{1,0:T(8,128)(2,1)}, b...) custom-call(bf16[1024,2048]{1,0:T(8,128)(2,1)} %add_convert_fusion.1.refs_0_, ...), custom_call_target="tpu_custom_call" | custom-call | tf_op jit(solution)/shard_map/reduce_all/pallas_call | solution.py:428
  476.4 0.8 slice_bitcast_fusion
  477.1 0.9 slice_bitcast_fusion.1
  478.1 0.8 slice.153
  478.8 6.8 %convert_element_type.210 = f32[1024,2048]{1,0:T(8,128)} convert(bf16[1024,2048]{1,0:T(8,128)(2,1)} %get-tuple-element.30) | non-fusion elementwise | flops 2097152 | bytes 12582912 | tf_op jit(solution)/shard_map/convert_element_type | solution.py:633
  485.6 4.4 convert_element_type.211
  490.1 3.5 convert_element_type.208
  493.6 1.6 convert_element_type.209
  499.3 3.3 fusion.56
  (149 shorter events, 9.0 us)
Async XLA Ops:
  0.6 98.3 %copy-start = (bf16[768,2048]{1,0:T(8,128)(2,1)S(1)}, bf16[768,2048]{1,0:T(8,128)(2,1)}, u32[]{:S(2)}) copy-start(bf16[768,2048]{1,0:T(8,128)(2,1)} %param.22) | copy-start | bytes 9437188
  93.5 3.5 copy-start.1
  93.5 4.7 copy-start.21
  93.5 4.7 copy-start.22
  98.2 6.6 %copy-start.27 = (f32[1024]{0:T(1024)}, f32[1024]{0:T(1024)S(1)}, u32[]{:S(2)}) copy-start(f32[1024]{0:T(1024)S(1)} %add_rsqrt_fusion) | copy-start | bytes 12292
  98.2 6.6 %copy-start.19 = (f32[2048]{0:T(1024)}, f32[2048]{0:T(1024)S(1)}, u32[]{:S(2)}) copy-start(f32[2048]{0:T(1024)S(1)} %convert_element_type.169) | copy-start | bytes 24580
  104.8 3.8 copy-start.29
  106.5 1.1 copy-start.9
  107.6 12.9 %copy-start.8 = (f32[1024,256]{0,1:T(8,128)S(1)}, f32[1024,256]{0,1:T(8,128)}, u32[]{:S(2)}) copy-start(f32[1024,256]{0,1:T(8,128)} %get-tuple-element.44) | copy-start | bytes 3145732
  108.6 0.9 copy-start.31
  113.3 81.0 %collective-permute-start = (bf16[1024,2,128]{0,2,1:T(8,128)(2,1)}, bf16[1024,2,128]{0,2,1:T(8,128)(2,1)}, u32[]{:S(2)}, u32[]{:S(2)}) collective-permute-start(bf16[1024,2,128]{0,2,1:T(8,128)(2,1)} %pad_maximum_fusion.2), channel_id=1, source_target_pairs={{0,0},{1,3},{2,6},{3,1},{4,4},{5,7},{6,2},{7,5},{8,8},{9,11},{10,1... | collective-permute-start | bytes 1572872 | tf_op jit(solution)/shard_map/ppermute | solution.py:514
  118.4 18.0 %copy-start.23 = (bf16[2048]{0:T(1024)(128)(2,1)S(1)}, bf16[2048]{0:T(1024)(128)(2,1)}, u32[]{:S(2)}) copy-start(bf16[2048]{0:T(1024)(128)(2,1)} %param.26) | copy-start | bytes 12292
  118.4 18.0 %copy-start.24 = (bf16[2048]{0:T(1024)(128)(2,1)S(1)}, bf16[2048]{0:T(1024)(128)(2,1)}, u32[]{:S(2)}) copy-start(bf16[2048]{0:T(1024)(128)(2,1)} %param.27) | copy-start | bytes 12292
  118.4 18.7 %copy-start.28 = (f32[1024]{0:T(1024)S(1)}, f32[1024]{0:T(1024)}, u32[]{:S(2)}) copy-start(f32[1024]{0:T(1024)} %copy-done.27) | copy-start | bytes 12292
  119.3 75.0 %collective-permute-start.1 = (bf16[1024,2,128]{0,2,1:T(8,128)(2,1)}, bf16[1024,2,128]{0,2,1:T(8,128)(2,1)}, u32[]{:S(2)}, u32[]{:S(2)}) collective-permute-start(bf16[1024,2,128]{0,2,1:T(8,128)(2,1)} %pad_maximum_fusion.3), channel_id=1, source_target_pairs={{0,1},{1,4},{2,7},{3,2},{4,5},{5,0},{6,3},{7,6},{8,9},{9,12},{10,1... | collective-permute-start | bytes 1572872 | tf_op jit(solution)/shard_map/ppermute | solution.py:514
  121.5 72.8 %collective-permute-start.2 = (bf16[1024,2,128]{0,2,1:T(8,128)(2,1)}, bf16[1024,2,128]{0,2,1:T(8,128)(2,1)}, u32[]{:S(2)}, u32[]{:S(2)}) collective-permute-start(bf16[1024,2,128]{0,2,1:T(8,128)(2,1)} %pad_maximum_fusion.4), channel_id=1, source_target_pairs={{0,2},{1,5},{2,0},{3,3},{4,6},{5,1},{6,4},{7,7},{8,10},{9,13},{10,... | collective-permute-start | bytes 1572872 | tf_op jit(solution)/shard_map/ppermute | solution.py:514
  129.1 83.8 %all-to-all-start = ((bf16[256,8,256]{0,2,1:T(8,128)(2,1)}), bf16[256,8,256]{0,2,1:T(8,128)(2,1)}, u32[]{:S(2)}, u32[]{:S(2)}) async-start(bf16[256,8,256]{0,2,1:T(8,128)(2,1)} %bitcast.153), calls=%async_computation | async-start | bytes 2097152 | tf_op jit(solution)/shard_map/all_to_all | solution.py:482
  137.2 16.7 %copy-start.34 = (bf16[1024,2048]{1,0:T(8,128)(2,1)S(1)}, bf16[1024,2048]{1,0:T(8,128)(2,1)}, u32[]{:S(2)}) copy-start(bf16[1024,2048]{1,0:T(8,128)(2,1)} %param.30) | copy-start | bytes 12582916
  137.2 16.7 %copy-start.35 = (bf16[1024,2048]{1,0:T(8,128)(2,1)S(1)}, bf16[1024,2048]{1,0:T(8,128)(2,1)}, u32[]{:S(2)}) copy-start(bf16[1024,2048]{1,0:T(8,128)(2,1)} %get-tuple-element.24) | copy-start | bytes 12582916
  153.9 6.1 %copy-start.33 = (bf16[1024,2048]{1,0:T(8,128)(2,1)S(1)}, bf16[1024,2048]{1,0:T(8,128)(2,1)}, u32[]{:S(2)}) copy-start(bf16[1024,2048]{1,0:T(8,128)(2,1)} %param.28) | copy-start | bytes 12582916
  160.0 6.7 %copy-start.2 = (bf16[1024,2048]{1,0:T(8,128)(2,1)S(1)}, bf16[1024,2048]{1,0:T(8,128)(2,1)}, u32[]{:S(2)}) copy-start(bf16[1024,2048]{1,0:T(8,128)(2,1)} %get-tuple-element.23) | copy-start | bytes 12582916
  180.5 6.4 %copy-start.30 = (s32[1,9]{1,0:T(1,128)S(1)}, s32[1,9]{1,0:T(1,128)}, u32[]{:S(2)}) copy-start(s32[1,9]{1,0:T(1,128)} %param.19) | copy-start | bytes 112
  180.5 6.4 %copy-start.32 = (s32[9]{0:T(128)S(1)}, s32[9]{0:T(128)}, u32[]{:S(2)}) copy-start(s32[9]{0:T(128)} %copy-done.31) | copy-start | bytes 112
  187.0 5.9 %copy-start.25 = (bf16[2048]{0:T(1024)(128)(2,1)S(1)}, bf16[2048]{0:T(1024)(128)(2,1)}, u32[]{:S(2)}) copy-start(bf16[2048]{0:T(1024)(128)(2,1)} %param.25) | copy-start | bytes 12292
  187.0 5.9 %copy-start.26 = (bf16[2048]{0:T(1024)(128)(2,1)S(1)}, bf16[2048]{0:T(1024)(128)(2,1)}, u32[]{:S(2)}) copy-start(bf16[2048]{0:T(1024)(128)(2,1)} %param.31) | copy-start | bytes 12292
  205.3 5.2 %copy-start.36 = (bf16[1024,2048]{1,0:T(8,128)(2,1)S(1)}, bf16[1024,2048]{1,0:T(8,128)(2,1)}, u32[]{:S(2)}) copy-start(bf16[1024,2048]{1,0:T(8,128)(2,1)} %get-tuple-element.24) | copy-start | bytes 12582916
  209.8 0.8 copy-start.14
  212.9 64.0 %all-to-all-start.1 = ((bf16[8,256,256]{2,1,0:T(8,128)(2,1)}), bf16[8,256,256]{2,1,0:T(8,128)(2,1)}, u32[]{:S(2)}, u32[]{:S(2)}) async-start(bf16[8,256,256]{2,1,0:T(8,128)(2,1)} %bitcast.165), calls=%async_computation.1 | async-start | bytes 2097152 | tf_op jit(solution)/shard_map/all_to_all | solution.py:568
  220.9 3.9 copy-start.5
  224.8 4.6 slice-start.2
  224.8 5.9 %slice-start.3 = ((s8[8388608]{0:T(1024)(128)(4,1)}), s8[4194304]{0:T(1024)(128)(4,1)S(1)}, s32[]{:S(2)}) async-start(s8[8388608]{0:T(1024)(128)(4,1)} %bitcast.146), calls=%async_computation.5 | async-start | bytes 8388608
  235.6 7.8 %slice-start = ((s8[8388608]{0:T(1024)(128)(4,1)}), s8[4194304]{0:T(1024)(128)(4,1)S(1)}, s32[]{:S(2)}) async-start(s8[8388608]{0:T(1024)(128)(4,1)} %bitcast.144), calls=%async_computation.2 | async-start | bytes 8388608
  235.6 1.6 copy-start.16
  235.6 1.6 copy-start.17
  235.6 7.7 %slice-start.1 = ((s8[8388608]{0:T(1024)(128)(4,1)}), s8[4194304]{0:T(1024)(128)(4,1)S(1)}, s32[]{:S(2)}) async-start(s8[8388608]{0:T(1024)(128)(4,1)} %bitcast.144), calls=%async_computation.3 | async-start | bytes 8388608
  237.3 6.0 %copy-start.7 = (bf16[8,256,256]{2,1,0:T(8,128)(2,1)S(1)}, bf16[8,256,256]{2,1,0:T(8,128)(2,1)}, u32[]{:S(2)}) copy-start(bf16[8,256,256]{2,1,0:T(8,128)(2,1)} %copy.87) | copy-start | bytes 3145732
  237.3 6.0 %copy-start.15 = (bf16[2,128,1024]{2,1,0:T(8,128)(2,1)S(1)}, bf16[2,128,1024]{2,1,0:T(8,128)(2,1)}, u32[]{:S(2)}) copy-start(bf16[2,128,1024]{2,1,0:T(8,128)(2,1)} %copy-done.14) | copy-start | bytes 1572868
  237.6 21.6 %slice-start.4 = ((s8[8388608]{0:T(1024)(128)(4,1)}), s8[4194304]{0:T(1024)(128)(4,1)S(1)}, s32[]{:S(2)}) async-start(s8[8388608]{0:T(1024)(128)(4,1)} %bitcast.182), calls=%async_computation.6 | async-start | bytes 8388608
  237.8 21.3 %collective-permute-start.3 = (bf16[1024,256]{0,1:T(8,128)(2,1)S(1)}, bf16[1024,256]{0,1:T(8,128)(2,1)S(1)}, u32[]{:S(2)}, u32[]{:S(2)}) collective-permute-start(bf16[1024,256]{0,1:T(8,128)(2,1)S(1)} %get-tuple-element.48), channel_id=1, source_target_pairs={{0,0},{3,1},{6,2},{1,3},{4,4},{7,5},{2,6},{5,7},{8,8},{11,9},{14,1... | collective-permute-start | bytes 1572872 | tf_op jit(solution)/shard_map/ppermute | solution.py:563
  240.4 18.7 %collective-permute-start.4 = (bf16[1024,256]{0,1:T(8,128)(2,1)S(1)}, bf16[1024,256]{0,1:T(8,128)(2,1)S(1)}, u32[]{:S(2)}, u32[]{:S(2)}) collective-permute-start(bf16[1024,256]{0,1:T(8,128)(2,1)S(1)} %get-tuple-element.47), channel_id=1, source_target_pairs={{1,0},{4,1},{7,2},{2,3},{5,4},{0,5},{3,6},{6,7},{9,8},{12,9},{15,1... | collective-permute-start | bytes 1572872 | tf_op jit(solution)/shard_map/ppermute | solution.py:563
  242.5 16.7 %copy-start.3 = (bf16[1024,2048]{1,0:T(8,128)(2,1)S(1)}, bf16[1024,2048]{1,0:T(8,128)(2,1)}, u32[]{:S(2)}) copy-start(bf16[1024,2048]{1,0:T(8,128)(2,1)} %get-tuple-element.23) | copy-start | bytes 12582916
  242.5 16.7 %slice-start.5 = ((s8[8388608]{0:T(1024)(128)(4,1)}), s8[4194304]{0:T(1024)(128)(4,1)S(1)}, s32[]{:S(2)}) async-start(s8[8388608]{0:T(1024)(128)(4,1)} %bitcast.182), calls=%async_computation.7 | async-start | bytes 8388608
  242.5 16.6 %collective-permute-start.5 = (bf16[1024,256]{0,1:T(8,128)(2,1)S(1)}, bf16[1024,256]{0,1:T(8,128)(2,1)S(1)}, u32[]{:S(2)}, u32[]{:S(2)}) collective-permute-start(bf16[1024,256]{0,1:T(8,128)(2,1)S(1)} %get-tuple-element.46), channel_id=1, source_target_pairs={{2,0},{5,1},{0,2},{3,3},{6,4},{1,5},{4,6},{7,7},{10,8},{13,9},{8,1... | collective-permute-start | bytes 1572872 | tf_op jit(solution)/shard_map/ppermute | solution.py:563
  259.2 8.4 %copy-start.11 = (bf16[1024,768]{0,1:T(8,128)(2,1)}, bf16[1024,768]{0,1:T(8,128)(2,1)S(1)}, u32[]{:S(2)}) copy-start(bf16[1024,768]{0,1:T(8,128)(2,1)S(1)} %constant_dynamic-update-slice_fusion) | copy-start | bytes 4718596
  259.2 9.7 %copy-start.20 = (f32[2048]{0:T(1024)S(1)}, f32[2048]{0:T(1024)}, u32[]{:S(2)}) copy-start(f32[2048]{0:T(1024)} %copy-done.19) | copy-start | bytes 24580
  478.8 6.8 %copy-start.6 = (bf16[1024,2048]{1,0:T(8,128)(2,1)S(1)}, bf16[1024,2048]{1,0:T(8,128)(2,1)}, u32[]{:S(2)}) copy-start(bf16[1024,2048]{1,0:T(8,128)(2,1)} %get-tuple-element.31) | copy-start | bytes 12582916
  485.6 4.5 copy-start.10
  490.1 3.6 copy-start.13
  490.1 5.1 %copy-start.4 = (bf16[1,128,2048]{2,1,0:T(8,128)(2,1)S(1)}, bf16[1,128,2048]{2,1,0:T(8,128)(2,1)}, u32[]{:S(2)}) copy-start(bf16[1,128,2048]{2,1,0:T(8,128)(2,1)} %param.16) | copy-start | bytes 1572868
  490.1 5.1 %copy-start.12 = (bf16[128,2048]{1,0:T(8,128)(2,1)S(1)}, bf16[128,2048]{1,0:T(8,128)(2,1)}, u32[]{:S(2)}) copy-start(bf16[128,2048]{1,0:T(8,128)(2,1)} %get-tuple-element.26) | copy-start | bytes 1572868
  496.2 6.9 %copy-start.18 = (f32[1,8,2,128]{3,1,2,0:T(8,128)}, f32[1,8,2,128]{3,1,2,0:T(8,128)S(1)}, u32[]{:S(2)}) copy-start(f32[1,8,2,128]{3,1,2,0:T(8,128)S(1)} %copy.124) | copy-start | bytes 24580
